TPU v7x, 256 devices: a whole 4x4x8 slice. The times are simulated.
256 devices in a mesh: seq: 64 (over z, y, core), head: 4 (over x).
Axes of the slice: x: 4, y: 4, z: 8, core: 2. Of those that a mesh axis runs over, the one named last changes fastest.
Arguments:
- q_in: bfloat16 [8192, 2048], P('seq', 'head'), may hold values from -6 to 6
- k_in: bfloat16 [8192, 2048], P('seq', 'head'), may hold values from -6 to 6
- v_in: bfloat16 [8192, 4096], P('seq', 'head'), may hold values from -6 to 6
- z_gate: bfloat16 [8192, 4096], P('seq', 'head'), may hold values from -6 to 6
- decay: float32 [8192, 32], P('seq', 'head'), may hold values from -1.5 to 0, as said below
- rate: float32 [8192, 32], P('seq', 'head'), may hold values from 0 to 0.95, as said below
- conv_q: float32 [4, 2048], P(None, 'head'), may hold values from -3 to 3
- conv_k: float32 [4, 2048], P(None, 'head'), may hold values from -3 to 3
- conv_v: float32 [4, 4096], P(None, 'head'), may hold values from -3 to 3
- norm_gain: float32 [128], replicated, may hold values from 0.5 to 1.5
- w_out: bfloat16 [4096, 2048], P('head'), may hold values from -0.09375 to 0.09375
Outputs:
- mixed: bfloat16 [8192, 2048], P('seq', 'head')
Inputs may be any that keep to these rules, and one draw needn't show every extreme that they name: `decay`: every entry is negative. `rate`: every entry is positive.
All inputs are finite; a program needn't handle non-finite values.
Results may differ from a plain program's by a relative error of at most 0.0049.
Values may be sent and summed in bfloat16 or wider, within the bound.
A program may use at most 192 MiB of HBM per device.

v0:
```python
import jax
import jax.numpy as jnp
from jax import lax
from jax.sharding import PartitionSpec as P

HEAD_DIM = 128
GROUP = 64


def shifted(shard, axis, by):
    size = lax.axis_size(axis)
    pairs = [(i, i + by) for i in range(size) if 0 <= i + by < size]
    return lax.ppermute(shard, axis, pairs)


def carried_in(part, axis, combine, identity):
    place = lax.axis_index(axis)
    gathered = jax.tree.map(lambda a: lax.all_gather(a, axis), part)
    state = jax.tree.map(lambda a, e: jnp.zeros_like(a) + jnp.asarray(e, a.dtype), part, identity)

    def one(lap, state):
        return combine(
            state, jax.tree.map(lambda a: lax.dynamic_index_in_dim(a, lap, 0, False), gathered)
        )

    return lax.fori_loop(0, place, one, state)


def combine_maps(earlier, later):
    highest = lax.Precision.HIGHEST
    first_a, first_b = earlier
    second_a, second_b = later
    joined_a = jnp.einsum("hij,hjk->hik", second_a, first_a, precision=highest)
    joined_b = jnp.einsum("hij,hjk->hik", second_a, first_b, precision=highest) + second_b
    return (joined_a, joined_b)


def on_device(q_in, k_in, v_in, z_gate, decay, rate, conv_q, conv_k, conv_v, norm_gain, w_out):
    highest = lax.Precision.HIGHEST
    tok = q_in.shape[0]
    key_cols = q_in.shape[1]
    val_cols = v_in.shape[1]
    key_heads = key_cols // HEAD_DIM
    val_heads = val_cols // HEAD_DIM
    blocks = tok // GROUP
    stacked = jnp.concatenate([q_in, k_in, v_in], axis=1)
    rim = shifted(stacked[tok - 3 :], "seq", 1)
    extended = jnp.concatenate([rim, stacked], axis=0).astype(jnp.float32)
    taps = jnp.concatenate([conv_q, conv_k, conv_v], axis=1)
    filtered = taps[0] * extended[0:tok]
    filtered = filtered + taps[1] * extended[1 : tok + 1]
    filtered = filtered + taps[2] * extended[2 : tok + 2]
    filtered = filtered + taps[3] * extended[3 : tok + 3]
    active = jax.nn.silu(filtered)
    query = active[:, :key_cols].reshape(tok, key_heads, HEAD_DIM)
    keys = active[:, key_cols : 2 * key_cols].reshape(tok, key_heads, HEAD_DIM)
    values = active[:, 2 * key_cols :].reshape(tok, val_heads, HEAD_DIM)
    query = (
        query
        * lax.rsqrt(jnp.sum(query * query, axis=-1, keepdims=True) + 1e-06)
        * HEAD_DIM ** (-0.5)
    )
    keys = keys * lax.rsqrt(jnp.sum(keys * keys, axis=-1, keepdims=True) + 1e-06)
    repeat = val_heads // key_heads
    query = jnp.repeat(query, repeat, axis=1)
    keys = jnp.repeat(keys, repeat, axis=1)

    def to_blocks(array):
        return array.reshape(blocks, GROUP, val_heads, HEAD_DIM).transpose(2, 0, 1, 3)

    q_blk = to_blocks(query)
    k_blk = to_blocks(keys)
    v_blk = to_blocks(values)
    log_decay = decay.reshape(blocks, GROUP, val_heads).transpose(2, 0, 1)
    strength = rate.reshape(blocks, GROUP, val_heads).transpose(2, 0, 1)
    cumulative = jnp.cumsum(log_decay, axis=-1)
    spread = cumulative[..., :, None] - cumulative[..., None, :]
    position = jnp.arange(GROUP)
    strict = position[:, None] > position[None, :]
    inclusive = position[:, None] >= position[None, :]
    below = jnp.where(strict, jnp.exp(jnp.where(strict, spread, 0.0)), 0.0)
    within = jnp.where(inclusive, jnp.exp(jnp.where(inclusive, spread, 0.0)), 0.0)
    key_key = jnp.einsum("hncd,hnsd->hncs", k_blk, k_blk, precision=highest)
    query_key = jnp.einsum("hncd,hnsd->hncs", q_blk, k_blk, precision=highest)
    system = jnp.eye(GROUP, dtype=jnp.float32) + strength[..., :, None] * below * key_key
    growth = jnp.exp(cumulative)
    tail = jnp.exp(cumulative[..., -1:] - cumulative)
    targets = jnp.concatenate(
        [strength[..., None] * v_blk, (strength * growth)[..., None] * k_blk], axis=-1
    )
    solved = lax.linalg.triangular_solve(
        system, targets, left_side=True, lower=True, unit_diagonal=True
    )
    w_value = solved[..., :HEAD_DIM]
    w_key = solved[..., HEAD_DIM:]
    weighted = tail[..., None] * k_blk
    identity = jnp.eye(HEAD_DIM, dtype=jnp.float32)
    block_a = jnp.exp(cumulative[..., -1])[..., None, None] * identity
    block_a = block_a - jnp.einsum("hncd,hnce->hnde", weighted, w_key, precision=highest)
    block_b = jnp.einsum("hncd,hnce->hnde", weighted, w_value, precision=highest)
    scores = within * query_key
    response = growth[..., None] * q_blk - jnp.einsum(
        "hncs,hnsd->hncd", scores, w_key, precision=highest
    )
    direct = jnp.einsum("hncs,hnse->hnce", scores, w_value, precision=highest)
    lead_a = block_a.transpose(1, 0, 2, 3)
    lead_b = block_b.transpose(1, 0, 2, 3)
    lead_resp = response.transpose(1, 0, 2, 3)
    lead_direct = direct.transpose(1, 0, 2, 3)
    start_a = jnp.broadcast_to(identity, (val_heads, HEAD_DIM, HEAD_DIM))
    start_b = jnp.zeros((val_heads, HEAD_DIM, HEAD_DIM), jnp.float32)

    def fold_blocks(carry, inputs):
        run_a, run_b = carry
        one_a, one_b = inputs
        next_a = jnp.einsum("hij,hjk->hik", one_a, run_a, precision=highest)
        next_b = jnp.einsum("hij,hjk->hik", one_a, run_b, precision=highest) + one_b
        return ((next_a, next_b), None)

    (shard_a, shard_b), _ = lax.scan(fold_blocks, (start_a, start_b), (lead_a, lead_b))
    prefix_maps = carried_in((shard_a, shard_b), "seq", combine_maps, (start_a, start_b))
    incoming = prefix_maps[1]

    def replay(state, inputs):
        one_a, one_b, one_resp, one_direct = inputs
        produced = jnp.einsum("hcd,hde->hce", one_resp, state, precision=highest) + one_direct
        state = jnp.einsum("hij,hjk->hik", one_a, state, precision=highest) + one_b
        return (state, produced)

    _, outputs = lax.scan(replay, incoming, (lead_a, lead_b, lead_resp, lead_direct))
    heads_out = outputs.transpose(0, 2, 1, 3).reshape(tok, val_heads, HEAD_DIM)
    scale = lax.rsqrt(jnp.mean(heads_out * heads_out, axis=-1, keepdims=True) + 1e-06)
    gate = jax.nn.silu(z_gate.astype(jnp.float32).reshape(tok, val_heads, HEAD_DIM))
    gated = (heads_out * scale * norm_gain * gate).astype(jnp.bfloat16).reshape(tok, val_cols)
    summed = lax.psum_scatter(
        lax.dot_general(w_out, gated, (((0,), (1,)), ((), ())), preferred_element_type=jnp.float32),
        "head",
        scatter_dimension=0,
        tiled=True,
    )
    return summed.T.astype(jnp.bfloat16)


def solution(mesh):
    return jax.shard_map(
        on_device,
        mesh=mesh,
        in_specs=(
            P("seq", "head"),
            P("seq", "head"),
            P("seq", "head"),
            P("seq", "head"),
            P("seq", "head"),
            P("seq", "head"),
            P(None, "head"),
            P(None, "head"),
            P(None, "head"),
            P(),
            P("head", None),
        ),
        out_specs=P("seq", "head"),
        check_vma=False,
    )
```

profile of v0, /device:TPU:161, one launch (start us, length us, event | category | flops | bytes accessed | tf_op | source)
XLA Modules:
  0.0 559.3 jit_solution(3943269036753793773)
XLA Ops:
  9.4 3.8 collective-permute-start
  21.1 78.6 %custom-call.3 = f32[8,2,1,64,64]{3,4,2,1,0:T(8,128)S(1)} custom-call(f32[8,2,1,64,64]{4,3,2,1,0:T(8,128)S(1)} %fusion.27), custom_call_target="InvertDiagBlocksLowerTriangular" | custom-call | tf_op jit(solution)/shard_map/triangular_solve | solution.py:91
  101.2 2.0 convolution_bitcast_fusion.1
  103.3 2.1 fusion.22
  105.5 2.9 while.39
  111.9 2.0 convolution_multiply_fusion
  116.9 133.9 %all-gather.5.cloned.1.call-done = f32[512,128,128]{2,1,0:T(8,128)} async-done(((f32[8,128,128]{2,1,0:T(8,128)}), f32[512,128,128]{2,1,0:T(8,128)}) %all-gather.5.cloned.1.call-update) | async-done | bytes 33554448 | tf_op jit(solution)/shard_map/all_gather | solution.py:18
  250.8 142.3 %all-gather.7.cloned.1.call-done = f32[512,128,128]{2,1,0:T(8,128)} async-done(((f32[8,128,128]{2,1,0:T(8,128)}), f32[512,128,128]{2,1,0:T(8,128)}) %all-gather.7.cloned.1.call-update) | async-done | bytes 33554448 | tf_op jit(solution)/shard_map/all_gather | solution.py:18
  393.1 80.7 %while.37 = (s32[]{:T(128)}, f32[8,128,128]{2,1,0:T(8,128)S(1)}, s32[]{:T(128)}, f32[64,8,128,128]{3,2,1,0:T(8,128)}, f32[64,8,128,128]{3,2,1,0:T(8,128)}, /*index=5*/s32[]{:T(128)}, s32[]{:T(128)}, s32[]{:T(128)}) while((s32[]{:T(128)}, f32[8,128,128]{2,1,0:T(8,128)S(1)}, s32[]{:T(128)}, f32[64,8,128,128]{3,2,1,0:T(8,128)}, ...), condition=%wide.region_5.6_spmd, body=%wide.region_4.5_spmd.sunk | while | flops 201457664 | bytes 3146871 | solution.py:26
  393.2 1.9 convolution_add_fusion.7
  397.2 1.9 convolution_add_fusion.7
  407.0 1.9 convolution_add_fusion.7
  414.9 1.9 convolution_add_fusion.7
  416.9 1.9 convolution_add_fusion.7
  424.7 1.9 convolution_add_fusion.7
  426.7 1.9 convolution_add_fusion.7
  434.6 1.9 convolution_add_fusion.7
  444.4 1.9 convolution_add_fusion.7
  452.2 1.9 convolution_add_fusion.7
  473.8 6.1 %while.38 = (s32[]{:T(128)}, f32[8,128,128]{2,1,0:T(8,128)S(1)}, f32[2,8,64,128]{3,2,1,0:T(8,128)}, f32[2,8,128,128]{3,2,1,0:T(8,128)S(1)}, f32[2,8,128,128]{3,2...) while((s32[]{:T(128)}, f32[8,128,128]{2,1,0:T(8,128)S(1)}, ...), condition=%wide.region_8.9_spmd, body=%wide.region_7.8_spmd.sunk | while | flops 302186496 | bytes 4458581 | solution.py:130
  473.9 2.3 fusion.94
  476.9 2.3 fusion.94
  482.9 4.1 convolution_bitcast_fusion
  487.0 64.2 %reduce-scatter.2.cloned.1.call-done = f32[512,128]{0,1:T(8,128)} async-done(((f32[2048,128]{0,1:T(8,128)}), f32[512,128]{0,1:T(8,128)}) %reduce-scatter.2.cloned.1.call-update) | async-done | bytes 262160 | tf_op jit(solution)/shard_map/reduce_scatter | solution.py:135
  (171 shorter events, 87.4 us)
Async XLA Ops:
  6.5 103.8 %copy-start = (f32[128]{0:T(128)S(1)}, f32[128]{0:T(128)}, u32[]{:S(2)}) copy-start(f32[128]{0:T(128)} %param.26) | copy-start | bytes 1540
  6.5 244.2 %all-gather.5.cloned.1.call-start = ((), (), s32[]{:S(2)}) async-start(), calls=%async_computation.2 | async-start | bytes 34078720 | tf_op jit(solution)/shard_map/all_gather | solution.py:18
  9.4 8.4 %collective-permute-start = (bf16[3,2048]{1,0:T(4,128)(2,1)S(1)}, bf16[3,2048]{1,0:T(4,128)(2,1)S(1)}, u32[]{:S(2)}, u32[]{:S(2)}) collective-permute-start(bf16[3,2048]{1,0:T(4,128)(2,1)S(1)} %slice.67), channel_id=1, source_target_pairs={{0,4},{4,8},{8,12},{12,16},{16,20},{20,24},{24,28},{28,32},{32,36}... | collective-permute-start | bytes 36872 | tf_op jit(solution)/shard_map/ppermute | solution.py:13
  20.1 83.2 %copy-start.4 = (f32[128,4,2,128]{3,0,2,1:T(8,128)}, f32[128,4,2,128]{3,0,2,1:T(8,128)S(1)}, u32[]{:S(2)}) copy-start(f32[128,4,2,128]{3,0,2,1:T(8,128)S(1)} %broadcast_in_dim.59) | copy-start | bytes 1572868
  101.2 4.3 copy-start.5
  108.4 0.8 copy-start.2
  108.4 1.0 copy-start.3
  109.3 283.8 %all-gather.7.cloned.1.call-start = ((), (), s32[]{:S(2)}) async-start(), calls=%async_computation.3 | async-start | bytes 34078720 | tf_op jit(solution)/shard_map/all_gather | solution.py:18
  110.0 3.9 copy-start.6
  110.0 441.2 %reduce-scatter.2.cloned.1.call-start = ((), (), s32[]{:S(2)}) async-start(), calls=%async_computation.1 | async-start | bytes 1310720 | tf_op jit(solution)/shard_map/reduce_scatter | solution.py:135
  393.1 80.7 %copy-start.7 = (f32[2,8,64,128]{3,2,0,1:T(8,128)S(1)}, f32[2,8,64,128]{3,2,0,1:T(8,128)}, u32[]{:S(2)}) copy-start(f32[2,8,64,128]{3,2,0,1:T(8,128)} %convolution_bitcast_fusion.3) | copy-start | bytes 1572868
  473.8 9.0 %copy-start.8 = (bf16[128,1024]{1,0:T(8,128)(2,1)S(1)}, bf16[128,1024]{1,0:T(8,128)(2,1)}, u32[]{:S(2)}) copy-start(bf16[128,1024]{1,0:T(8,128)(2,1)} %param.20) | copy-start | bytes 786436
  482.6 70.2 %copy-start.1 = (f32[128]{0:T(128)S(1)}, f32[128]{0:T(128)}, u32[]{:S(2)}) copy-start(f32[128]{0:T(128)} %param.26) | copy-start | bytes 1540
Sparse Core Ops, SparseCore 0:
  109.4 141.3 all-gather.4
  253.6 139.5 all-gather.6
  487.1 64.0 reduce-scatter.1
where the time goes:
time: 565 us; the launch traced here: 559 us
  waiting for transfers between devices  341 us (60%)
  matrix products  101 us (18%)
  other arithmetic  84.1 us (15%)
  between operations  13.6 us (2%)
  local copies, waits for them, and re-layouts  13.4 us (2%)
    all_gather x2, waiting for transfers between devices, carried_in(): gathered = jax.tree.map(lambda a: lax.all_gather(a, axis), part)  276 us
    another operation x2, other arithmetic, on_device(): lax.linalg.triangular_solve(system, targets, left_side=True, lower=True,...  78.6 us
    dot_general x41, matrix products, combine_maps(): jnp.einsum('hij,hjk->hik', second_a, first_b, precision=highest) + second_b  77.6 us
    reduce_scatter x1, waiting for transfers between devices, on_device(): lax.psum_scatter(lax.dot_general(w_out, gated, (((0,), (1,)), ((), ())),...  64.2 us
  transfers between devices with their start and end apart: 4, of which 3 were waited for; matrix products, arithmetic and copies ran while one was open for 2% of the time, Pallas kernels for 0%

commit v1 on v0

v1 whole, which is shorter than its diff:
```python
import jax
import jax.numpy as jnp
from jax import lax
from jax.experimental import pallas as pl
from jax.experimental.pallas import tpu as pltpu
from jax.sharding import PartitionSpec as P

F32 = jnp.float32
BF16 = jnp.bfloat16
D = 128
PLANE = 8
PLANES = 8
HEADS_X = 4
MESH = pl.DeviceIdType.MESH
VMEM = pltpu.VMEM


def split(x):
    high = x.astype(BF16)
    return high, (x - high.astype(F32)).astype(BF16)


def left(x):
    high, low = split(x)
    return jnp.concatenate([high, low], axis=1)


def right(x):
    high, low = split(x)
    both = jnp.concatenate([high, low], axis=1)
    return jnp.concatenate([both, both], axis=0)


def product(lhs, rhs):
    both = jnp.dot(lhs, rhs, preferred_element_type=F32)
    half = both.shape[1] // 2
    return both[:, :half] + both[:, half:]


def silu(x):
    return x / (1.0 + jnp.exp(-x))


def iotas():
    return lax.broadcasted_iota(jnp.int32, (D, D), 0), lax.broadcasted_iota(jnp.int32, (D, D), 1)


def chunk_maps(query, keys, values, gates):
    row, col = iotas()
    rates = gates[1:2, :]
    upper = (row <= col).astype(BF16)
    high = gates.astype(BF16)
    rest = gates - high.astype(F32)
    mid = rest.astype(BF16)
    low = (rest - mid.astype(F32)).astype(BF16)
    sums = jnp.dot(jnp.concatenate([high, mid, low], axis=0), upper, preferred_element_type=F32)
    sums = sums[0:8] + sums[8:16] + sums[16:24]
    cum_row = sums[0:1, :]
    rows = jnp.concatenate([cum_row, rates, jnp.zeros((D - 2, D), F32)], axis=0)
    cols = rows.T
    cum_col = jnp.broadcast_to(cols[:, 0:1], (D, D))
    rate_col = jnp.broadcast_to(cols[:, 1:2], (D, D))
    spread = cum_col - cum_row
    inclusive = row >= col
    within = jnp.where(inclusive, jnp.exp(jnp.where(inclusive, spread, 0.0)), 0.0)
    keys_t = keys.T
    both = product(jnp.concatenate([left(query), left(keys)], axis=0), right(keys_t))
    query_key, key_key = both[:D], both[D:]
    scores = within * query_key
    system = jnp.where(row > col, rate_col * within * key_key, 0.0)
    differ = row ^ col
    inverse = jnp.where(row == col, 1.0, jnp.where(differ == 1, -system, 0.0))
    for level in range(1, 7):
        part = jnp.where((differ >= (1 << level)) & (differ < (2 << level)), system, 0.0)
        inner = product(left(part), right(inverse))
        inverse = inverse - product(left(inverse), right(inner))
    growth = jnp.exp(cum_col)
    targets = jnp.concatenate([(rate_col * growth) * keys, rate_col * values], axis=1)
    solved = product(left(inverse), right(targets))
    solved_right = right(solved)
    tail_row = jnp.exp(cum_col[D - 1 : D, :] - cum_row)
    weighted_t = keys_t * tail_row
    inside = product(left(weighted_t), solved_right)
    whole = jnp.where(row == col, growth[D - 1 : D, :], 0.0)
    maps = jnp.concatenate([whole - inside[:, :D], inside[:, D:]], axis=1)
    seen = product(left(scores), solved_right)
    response = growth * query - seen[:, :D]
    return maps, response, seen[:, D:]


def compose(later, earlier):
    joined = product(left(later[:, :D]), right(earlier))
    return jnp.concatenate([joined[:, :D], joined[:, D:] + later[:, D:]], axis=1)


def kernel(
    q_ref, k_ref, v_ref, z_ref, gate_ref, cq_ref, ck_ref, cv_ref, gain_ref, w_ref, out_ref,
    raw, gates, halo, ext, act, maps, resp, direct, mine, got, own, back, whole, w_all, x_send, x_got,
    send_raw, recv_raw, send_gate, recv_gate, send_halo, recv_halo, send_z, recv_z,
    send_back, recv_back, send_x, recv_x, w_sem,
):
    me, head = lax.axis_index("seq"), lax.axis_index("head")
    plane, place = me // PLANE, lax.rem(me, PLANE)
    first = plane * PLANE

    def peer(r):
        return lax.rem(place + r, PLANE)

    def plane_at(r):
        return lax.rem(plane + r + PLANES, PLANES) * PLANE + place

    barrier = pltpu.get_barrier_semaphore()
    near = [(first + peer(r), head) for r in range(1, PLANE)]
    near += [(plane_at(r), head) for r in (1, -1, 2, -2, 4)]
    near += [(me, lax.rem(head + r, HEADS_X)) for r in range(1, HEADS_X)]
    for device in near:
        pl.semaphore_signal(barrier, inc=1, device_id=device, device_id_type=MESH)

    w_copy = pltpu.make_async_copy(w_ref, w_all, w_sem)
    w_copy.start()
    sources = (k_ref, q_ref, v_ref, z_ref)

    def columns(a, dest):
        return pl.ds(pl.multiple_of((dest // 2 if a < 2 else dest) * D, D), D)

    kept = []
    for a in range(4):
        copy = pltpu.make_async_copy(
            sources[a].at[:, columns(a, place)], raw.at[a, place], recv_raw.at[a, place]
        )
        copy.start()
        kept.append(copy)
    gates[place] = gate_ref[place]

    pl.semaphore_wait(barrier, len(near))

    sent = []

    def send(src, dst, send_sem, recv_sem, device):
        copy = pltpu.make_async_remote_copy(
            src_ref=src, dst_ref=dst, send_sem=send_sem, recv_sem=recv_sem, device_id=device, device_id_type=MESH
        )
        copy.start()
        sent.append(copy)
        return copy

    def arrived(dst, send_sem, recv_sem):
        pltpu.make_async_remote_copy(
            src_ref=dst, dst_ref=dst, send_sem=send_sem, recv_sem=recv_sem, device_id=near[0], device_id_type=MESH
        ).wait_recv()

    for a in range(4):
        for r in range(1, PLANE):
            dest = peer(r)
            send(
                sources[a].at[:, columns(a, dest)], raw.at[a, place],
                send_raw.at[a, r - 1], recv_raw.at[a, place], (first + dest, head),
            )
        if a == 0:
            for r in range(1, PLANE):
                dest = peer(r)
                send(
                    gate_ref.at[dest], gates.at[place],
                    send_gate.at[r - 1], recv_gate.at[place], (first + dest, head),
                )

    taps = [
        ck_ref[:, columns(0, place)],
        cq_ref[:, columns(0, place)],
        cv_ref[:, columns(2, place)],
    ]

    def activate(a, before, now):
        ext[a, 0:8, :] = before.astype(F32)[8:16]
        ext[a, 8 : 8 + D, :] = now.astype(F32)
        total = taps[a][0:1] * ext[a, 5 : 5 + D, :]
        for t in range(1, 4):
            total = total + taps[a][t : t + 1] * ext[a, 5 + t : 5 + t + D, :]
        total = silu(total)
        if a < 2:
            total = total * lax.rsqrt(jnp.sum(total * total, axis=-1, keepdims=True) + 1e-06)
        if a == 1:
            total = total * D ** (-0.5)
        return total

    for a in range(4):
        kept[a].wait()
    for a in range(3):
        for r in range(1, PLANE):
            src = peer(r)
            arrived(raw.at[a, src], send_raw.at[a, 0], recv_raw.at[a, src])
        send(
            raw.at[a, PLANE - 1, D - 16 : D, :], halo.at[a], send_halo.at[a], recv_halo.at[a], (plane_at(1), head)
        )

    @pl.loop(1, PLANE)
    def _(n):
        for a in range(3):
            act[a, n] = activate(a, raw[a, n - 1, D - 16 : D, :], raw[a, n])

    for a in range(3):
        arrived(halo.at[a], send_halo.at[a], recv_halo.at[a])
        before = jnp.where(plane > 0, halo[a], jnp.zeros_like(halo[a]))
        act[a, 0] = activate(a, before, raw[a, 0])
    for r in range(1, PLANE):
        src = peer(r)
        arrived(gates.at[src], send_gate.at[0], recv_gate.at[src])

    @pl.loop(0, PLANE // 4)
    def _(t):
        for u in range(4):
            n = t * 4 + u
            maps[n], resp[n], direct[n] = chunk_maps(act[1, n], act[0, n], act[2, n], gates[n])

    joined = {}
    joined[0, 1] = compose(maps[1], maps[0])
    joined[2, 3] = compose(maps[3], maps[2])
    joined[4, 5] = compose(maps[5], maps[4])
    joined[6, 7] = compose(maps[7], maps[6])
    joined[0, 3] = compose(joined[2, 3], joined[0, 1])
    joined[4, 7] = compose(joined[6, 7], joined[4, 5])
    total = compose(joined[4, 7], joined[0, 3])

    mine[0] = total
    send(mine.at[0], got.at[0], send_z.at[0], recv_z.at[0], (plane_at(1), head))

    prefix = [None, maps[0], joined[0, 1], compose(maps[2], joined[0, 1]), joined[0, 3]]
    prefix.append(compose(maps[4], joined[0, 3]))
    prefix.append(compose(joined[4, 5], joined[0, 3]))
    prefix.append(compose(maps[6], prefix[6]))
    for n in range(1, PLANE):
        through = product(left(resp[n]), right(prefix[n]))
        resp[n] = through[:, :D]
        direct[n] = through[:, D:] + direct[n]

    def reached(slot, distance):
        arrived(got.at[slot], send_z.at[slot], recv_z.at[slot])
        return jnp.where(plane >= distance, got[slot], jnp.zeros_like(got[slot]))

    one = reached(0, 1)
    two = compose(total, one)
    mine[1] = two
    send(mine.at[1], got.at[1], send_z.at[1], recv_z.at[1], (plane_at(2), head))

    for r in range(1, PLANE):
        src = peer(r)
        arrived(raw.at[3, src], send_raw.at[3, 0], recv_raw.at[3, src])

    @pl.loop(0, PLANE)
    def _(n):
        own[n] = silu(raw[3, n].astype(F32)) * gain_ref[...]

    before = reached(1, 2)
    four = product(left(two[:, :D]), right(before[:, D:])) + two[:, D:]
    mine[2, :, 0:D] = four
    send(
        mine.at[2, :, pl.ds(0, D)], got.at[2, :, pl.ds(0, D)], send_z.at[2], recv_z.at[2], (plane_at(4), head)
    )
    three = compose(one, before)
    arrived(got.at[2, :, pl.ds(0, D)], send_z.at[2], recv_z.at[2])
    far = jnp.where(plane >= 4, got[2, :, 0:D], 0.0)
    state = product(left(three[:, :D]), right(far)) + three[:, D:]
    state_right = right(state)

    for r in range(PLANE - 1, -1, -1):
        n = peer(r)
        heads_out = product(left(resp[n]), state_right) + direct[n]
        scale = lax.rsqrt(jnp.mean(heads_out * heads_out, axis=-1, keepdims=True) + 1e-06)
        gated = (heads_out * scale * own[n]).astype(BF16)
        lanes = pl.ds(pl.multiple_of(place * D, D), D)
        if r == 0:
            whole[:, lanes] = gated
        else:
            back[r - 1] = gated
            send(
                back.at[r - 1], whole.at[:, lanes], send_back.at[r - 1], recv_back.at[place], (first + n, head)
            )
    for r in range(1, PLANE):
        src = peer(r)
        arrived(whole.at[:, pl.ds(pl.multiple_of(src * D, D), D)], send_back.at[0], recv_back.at[src])
    w_copy.wait()

    width = out_ref.shape[1]
    for r in (2, 1, 3, 0):
        dest = lax.rem(head + r, HEADS_X)
        weights = w_all[:, pl.ds(pl.multiple_of(dest * width, width), width)]
        share = jnp.dot(whole[...], weights, preferred_element_type=F32)
        if r > 0:
            x_send[r - 1] = share.astype(BF16)
            send(x_send.at[r - 1], x_got.at[r - 1], send_x.at[r - 1], recv_x.at[r - 1], (me, dest))
    for r in (1, 3, 2):
        arrived(x_got.at[r - 1], send_x.at[r - 1], recv_x.at[r - 1])
        share = share + x_got[r - 1].astype(F32)
    out_ref[...] = share.astype(BF16)
    for copy in sent:
        copy.wait_send()


def on_device(q_in, k_in, v_in, z_gate, decay, rate, conv_q, conv_k, conv_v, norm_gain, w_out):
    heads = decay.shape[1]
    gate = jnp.stack([decay.T, rate.T] + [jnp.zeros((heads, D), F32)] * 6, axis=1)
    tok, width = q_in.shape
    any_space = pl.BlockSpec(memory_space=pl.ANY)
    vmem = pl.BlockSpec(memory_space=VMEM)
    dma = pltpu.SemaphoreType.DMA
    return pl.pallas_call(
        kernel,
        out_shape=jax.ShapeDtypeStruct((tok, width), BF16),
        in_specs=[any_space] * 4 + [vmem] * 5 + [any_space],
        out_specs=vmem,
        scratch_shapes=[
            VMEM((4, PLANE, D, D), BF16),
            VMEM((PLANE, 8, D), F32),
            VMEM((3, 16, D), BF16),
            VMEM((3, D + 8, D), F32),
            VMEM((3, PLANE, D, D), F32),
            VMEM((PLANE, D, 2 * D), F32),
            VMEM((PLANE, D, D), F32),
            VMEM((PLANE, D, D), F32),
            VMEM((3, D, 2 * D), F32),
            VMEM((3, D, 2 * D), F32),
            VMEM((PLANE, D, D), F32),
            VMEM((PLANE - 1, D, D), BF16),
            VMEM((tok, PLANE * D), BF16),
            VMEM(w_out.shape, BF16),
            VMEM((HEADS_X - 1, tok, width), BF16),
            VMEM((HEADS_X - 1, tok, width), BF16),
            dma((4, PLANE - 1)), dma((4, PLANE)),
            dma((PLANE - 1,)), dma((PLANE,)),
            dma((3,)), dma((3,)),
            dma((3,)), dma((3,)),
            dma((PLANE - 1,)), dma((PLANE,)),
            dma((HEADS_X - 1,)), dma((HEADS_X - 1,)),
            dma,
        ],
        compiler_params=pltpu.CompilerParams(
            collective_id=0, has_side_effects=True, vmem_limit_bytes=40 * 1024 * 1024
        ),
    )(q_in, k_in, v_in, z_gate, gate, conv_q, conv_k, conv_v, norm_gain.reshape(1, D), w_out)


def solution(mesh):
    return jax.shard_map(
        on_device,
        mesh=mesh,
        in_specs=(
            P("seq", "head"),
            P("seq", "head"),
            P("seq", "head"),
            P("seq", "head"),
            P("seq", "head"),
            P("seq", "head"),
            P(None, "head"),
            P(None, "head"),
            P(None, "head"),
            P(),
            P("head", None),
        ),
        out_specs=P("seq", "head"),
        check_vma=False,
    )
```

time: 565 us -> 88.8 us (0.16)
  the two profiles are of different devices: /device:TPU:161 before, /device:TPU:1 now
where the time goes in v1:
time: 88.8 us; the launch traced here: 88.4 us
  Pallas kernels  78.2 us (88%)
  local copies, waits for them, and re-layouts  9.47 us (11%)
    pallas_call x1, Pallas kernels, on_device(): pl.pallas_call(kernel, out_shape=jax.ShapeDtypeStruct((tok, width), BF16)...  78.2 us
    unnamed x19, local copies, waits for them, and re-layouts  9.32 us

profile of v1, /device:TPU:1, one launch (start us, length us, event | category | flops | bytes accessed | tf_op | source)
XLA Modules:
  0.0 88.4 jit_solution(8943640331500500825)
XLA Ops:
  0.0 0.1 pad.3.clone
  0.1 0.1 pad.2.clone
  0.2 0.8 maximum_maximum_fusion.gate_ref
  0.9 0.0 copy-start
  0.9 2.2 %copy-done = bf16[1024,2048]{1,0:T(8,128)(2,1)S(1)} copy-done((bf16[1024,2048]{1,0:T(8,128)(2,1)S(1)}, bf16[1024,2048]{1,0:T(8,128)(2,1)}, u32[]{:S(2)}) %copy-start) | copy-done | bytes 4194328
  3.1 0.0 copy-start.1
  3.1 0.9 %copy-done.1 = bf16[128,1024]{1,0:T(8,128)(2,1)S(1)} copy-done((bf16[128,1024]{1,0:T(8,128)(2,1)S(1)}, bf16[128,1024]{1,0:T(8,128)(2,1)}, u32[]{:S(2)}) %copy-start.1) | copy-done | bytes 262168
  4.1 0.0 copy-start.2
  4.1 0.9 %copy-done.2 = bf16[128,1024]{1,0:T(8,128)(2,1)S(1)} copy-done((bf16[128,1024]{1,0:T(8,128)(2,1)S(1)}, bf16[128,1024]{1,0:T(8,128)(2,1)}, u32[]{:S(2)}) %copy-start.2) | copy-done | bytes 262168
  5.0 0.0 copy-start.3
  5.0 0.9 %copy-done.3 = bf16[128,512]{1,0:T(8,128)(2,1)S(1)} copy-done((bf16[128,512]{1,0:T(8,128)(2,1)S(1)}, bf16[128,512]{1,0:T(8,128)(2,1)}, u32[]{:S(2)}) %copy-start.3) | copy-done | bytes 131096
  5.9 0.0 copy-start.4
  5.9 0.9 %copy-done.4 = bf16[128,512]{1,0:T(8,128)(2,1)S(1)} copy-done((bf16[128,512]{1,0:T(8,128)(2,1)S(1)}, bf16[128,512]{1,0:T(8,128)(2,1)}, u32[]{:S(2)}) %copy-start.4) | copy-done | bytes 131096
  6.8 0.0 copy-start.5
  6.8 0.7 copy-done.5
  7.6 0.0 copy-start.6
  7.6 0.7 copy-done.6
  8.3 0.0 copy-start.7
  8.3 0.7 copy-done.7
  8.9 0.0 copy-start.8
  8.9 0.7 copy-done.8
  9.6 78.2 %shard_map.109 = bf16[128,512]{1,0:T(8,128)(2,1)S(1)} custom-call(bf16[128,512]{1,0:T(8,128)(2,1)S(1)} %copy-done.3, bf16[128,512]{1,0:T(8,128)(2,1)S(1)} %copy-done.4, bf16[128,1024]{1,0:T(8,128)(2,1)S(1)} %copy-done.1, bf16[128,1024]{1,0:T(8,128)(2,1)S(1)} %copy-done.2, f32[8,8,128]{2,1,0:T(8,128)S(1)} %maximum_maximum_fusion.gate_ref, ...), custom_call_target="tpu_custom_call" | custom-call | tf_op jit(solution)/shard_map/pallas_call | solution.py:306
  87.8 0.7 copy.13
  (2 shorter events, 0.0 us)
Async XLA Ops:
  0.9 2.2 %copy-start = (bf16[1024,2048]{1,0:T(8,128)(2,1)S(1)}, bf16[1024,2048]{1,0:T(8,128)(2,1)}, u32[]{:S(2)}) copy-start(bf16[1024,2048]{1,0:T(8,128)(2,1)} %w_ref.1) | copy-start | bytes 12582916
  3.1 0.9 %copy-start.1 = (bf16[128,1024]{1,0:T(8,128)(2,1)S(1)}, bf16[128,1024]{1,0:T(8,128)(2,1)}, u32[]{:S(2)}) copy-start(bf16[128,1024]{1,0:T(8,128)(2,1)} %v_ref.1) | copy-start | bytes 786436
  4.1 0.9 %copy-start.2 = (bf16[128,1024]{1,0:T(8,128)(2,1)S(1)}, bf16[128,1024]{1,0:T(8,128)(2,1)}, u32[]{:S(2)}) copy-start(bf16[128,1024]{1,0:T(8,128)(2,1)} %z_ref.1) | copy-start | bytes 786436
  5.0 0.9 %copy-start.3 = (bf16[128,512]{1,0:T(8,128)(2,1)S(1)}, bf16[128,512]{1,0:T(8,128)(2,1)}, u32[]{:S(2)}) copy-start(bf16[128,512]{1,0:T(8,128)(2,1)} %q_ref.1) | copy-start | bytes 393220
  5.9 0.9 %copy-start.4 = (bf16[128,512]{1,0:T(8,128)(2,1)S(1)}, bf16[128,512]{1,0:T(8,128)(2,1)}, u32[]{:S(2)}) copy-start(bf16[128,512]{1,0:T(8,128)(2,1)} %k_ref.1) | copy-start | bytes 393220
  6.8 0.7 copy-start.5
  7.6 0.7 copy-start.6
  8.3 0.7 copy-start.7
  8.9 0.7 copy-start.8

commit v2 on v1

v2 whole, which is shorter than its diff:
```python
import jax
import jax.numpy as jnp
from jax import lax
from jax.experimental import pallas as pl
from jax.experimental.pallas import tpu as pltpu
from jax.sharding import PartitionSpec as P

F32 = jnp.float32
BF16 = jnp.bfloat16
D = 128
PLANE = 8
PLANES = 8
HEADS_X = 4
MESH = pl.DeviceIdType.MESH
VMEM = pltpu.VMEM


def split(x):
    high = x.astype(BF16)
    return high, (x - high.astype(F32)).astype(BF16)


def left(x):
    high, low = split(x)
    return jnp.concatenate([high, low], axis=1)


def right(x):
    high, low = split(x)
    both = jnp.concatenate([high, low], axis=1)
    return jnp.concatenate([both, both], axis=0)


def product(lhs, rhs):
    both = jnp.dot(lhs, rhs, preferred_element_type=F32)
    half = both.shape[1] // 2
    return both[:, :half] + both[:, half:]


def silu(x):
    return x / (1.0 + jnp.exp(-x))


def iotas(rows=D):
    return lax.broadcasted_iota(jnp.int32, (rows, D), 0), lax.broadcasted_iota(jnp.int32, (rows, D), 1)


def gate_tables(decays, rates):
    row, col = iotas()
    upper = (row <= col).astype(BF16)
    high, rest = split(decays)
    mid, low = split(decays - high.astype(F32))
    sums = jnp.dot(jnp.concatenate([high, mid, low], axis=0), upper, preferred_element_type=F32)
    sums = sums[0:PLANE] + sums[PLANE : 2 * PLANE] + sums[2 * PLANE : 3 * PLANE]
    table = jnp.concatenate([sums, rates, jnp.zeros((D - 2 * PLANE, D), F32)], axis=0)
    return sums, table.T


def inverses(systems):
    row, col = iotas()
    count = len(systems)
    diagonal = (row >> 4) == (col >> 4)
    packed = []
    for system in systems:
        blocks = jnp.where(diagonal, system, 0.0)
        rows = blocks[0:16]
        for b in range(1, 8):
            rows = rows + blocks[16 * b : 16 * b + 16]
        packed.append(rows)
    packed = left(jnp.concatenate(packed, axis=0))
    row16, col16 = iotas(16)
    eye = jnp.where(row16 == (col16 & 15), 1.0, 0.0)
    found = jnp.concatenate([eye] * count, axis=0).reshape(count, 16, D)
    same = (row >> 4) == (col >> 4)
    for first in range(0, 15, 2):
        picks = range(first, min(first + 2, 15))
        spread = [(same & ((row & 15) == j)).astype(BF16) for j in picks]
        spread = jnp.concatenate(spread, axis=1)
        spread = jnp.dot(packed, jnp.concatenate([spread, spread], axis=0), preferred_element_type=F32)
        for u, j in enumerate(picks):
            factor = spread[:, u * D : (u + 1) * D].reshape(count, 16, D)
            found = found - factor * found[:, j : j + 1, :]
    result = [jnp.where(diagonal, jnp.concatenate([found[n]] * 8, axis=0), 0.0) for n in range(count)]
    differ = row ^ col
    for level in range(4, 7):
        off = (differ >= (1 << level)) & (differ < (2 << level))
        parts = [left(jnp.where(off, system, 0.0)) for system in systems]
        inner = [product(parts[n], right(result[n])) for n in range(count)]
        result = [result[n] - product(left(result[n]), right(inner[n])) for n in range(count)]
    return result


def compose(later, earlier):
    d_later, both_later = later
    d_earlier, both_earlier = earlier
    joined = product(left(both_later[:, :D]), right(both_earlier))
    wide = jnp.concatenate([d_later, d_later], axis=1)
    factors = jnp.concatenate([d_earlier, jnp.ones_like(d_earlier)], axis=1)
    return d_later * d_earlier, joined + wide * both_earlier + factors * both_later


def kernel(
    q_ref, k_ref, v_ref, z_ref, decay_ref, rate_ref, cq_ref, ck_ref, cv_ref, gain_ref, w_ref, out_ref,
    raw, gate_own, gates, halo, ext, act, taps, gain, reach, direct, mine, got, own, back, whole, w_all, x_send, x_got,
    send_raw, recv_raw, send_gate, recv_gate, send_halo, recv_halo, send_z, recv_z,
    send_back, recv_back, send_x, recv_x, w_sem, small_sem,
):
    me, head = lax.axis_index("seq"), lax.axis_index("head")
    plane, place = me // PLANE, lax.rem(me, PLANE)
    first = plane * PLANE
    last = place == PLANE - 1

    def peer(r):
        return lax.rem(place + r, PLANE)

    def plane_at(r):
        return lax.rem(plane + r + PLANES, PLANES) * PLANE

    sources = (k_ref, v_ref, q_ref, z_ref)

    def columns(a, dest):
        return pl.ds(pl.multiple_of((dest if a % 2 else dest // 2) * D, D), D)

    small = [
        pltpu.make_async_copy(src, dst, small_sem.at[i])
        for i, (src, dst) in enumerate(
            [
                (decay_ref, gate_own.at[0:8]),
                (rate_ref, gate_own.at[8:16]),
                (ck_ref.at[:, columns(0, place)], taps.at[0]),
                (cv_ref.at[:, columns(1, place)], taps.at[1]),
                (cq_ref.at[:, columns(2, place)], taps.at[2]),
                (gain_ref, gain),
            ]
        )
    ]
    for copy in small:
        copy.start()

    barrier = pltpu.get_barrier_semaphore()
    near = [(first + peer(r), head) for r in range(1, PLANE)]
    near += [(plane_at(r) + place, head) for r in (1, -1, 2, -2, 4)]
    near += [(me, lax.rem(head + r, HEADS_X)) for r in range(1, HEADS_X)]
    for device in near:
        pl.semaphore_signal(barrier, inc=1, device_id=device, device_id_type=MESH)

    @pl.when(jnp.logical_not(last))
    def _():
        pl.semaphore_signal(barrier, inc=1, device_id=(plane_at(-1) + PLANE - 1, head), device_id_type=MESH)

    kept = []
    for a in range(4):
        copy = pltpu.make_async_copy(
            sources[a].at[:, columns(a, place)], raw.at[a, place], recv_raw.at[a, place]
        )
        copy.start()
        kept.append(copy)
    w_copy = pltpu.make_async_copy(w_ref, w_all, w_sem)
    w_copy.start()
    for copy in small[:2]:
        copy.wait()

    pl.semaphore_wait(barrier, len(near) + jnp.where(last, PLANE - 1, 0))

    sent = []

    def remote(src, dst, send_sem, recv_sem, device):
        return pltpu.make_async_remote_copy(
            src_ref=src, dst_ref=dst, send_sem=send_sem, recv_sem=recv_sem, device_id=device, device_id_type=MESH
        )

    def send(*args):
        copy = remote(*args)
        copy.start()
        sent.append(copy)

    def arrived(dst, send_sem, recv_sem):
        remote(dst, dst, send_sem, recv_sem, near[0]).wait_recv()

    def halo_copy(a, j):
        return remote(
            sources[a].at[D - 16 : D, columns(a, j)], halo.at[a],
            send_halo.at[a, j], recv_halo.at[a], (plane_at(1) + j, head),
        )

    for r in range(1, PLANE):
        dest = peer(r)
        send(gate_own, gates.at[place], send_gate.at[r - 1], recv_gate.at[place], (first + dest, head))
    for a in range(4):
        for r in range(1, PLANE):
            dest = peer(r)
            send(
                sources[a].at[:, columns(a, dest)], raw.at[a, place],
                send_raw.at[a, r - 1], recv_raw.at[a, place], (first + dest, head),
            )
        if a < 3:

            @pl.when(last)
            def _():
                for j in range(PLANE):
                    halo_copy(a, j).start()

    def raw_arrived(a):
        kept[a].wait()
        for r in range(1, PLANE):
            src = peer(r)
            arrived(raw.at[a, src], send_raw.at[a, 0], recv_raw.at[a, src])
        if a < 3:
            arrived(halo.at[a], send_halo.at[a, 0], recv_halo.at[a])

    def activate(a):
        before = jnp.where(plane > 0, halo[a].astype(F32), 0.0)
        ext[a, 0:8, :] = before[8:16]
        for n in range(PLANE):
            ext[a, 8 + n * D : 8 + (n + 1) * D, :] = raw[a, n].astype(F32)
        for n in range(PLANE):
            total = taps[a, 0:1] * ext[a, 5 + n * D : 5 + (n + 1) * D, :]
            for t in range(1, 4):
                total = total + taps[a, t : t + 1] * ext[a, 5 + t + n * D : 5 + t + (n + 1) * D, :]
            total = silu(total)
            if a != 1:
                total = total * lax.rsqrt(jnp.sum(total * total, axis=-1, keepdims=True) + 1e-06)
            if a == 2:
                total = total * D ** (-0.5)
            act[a, n] = total

    gates[place] = gate_own[...]
    for r in range(1, PLANE):
        src = peer(r)
        arrived(gates.at[src], send_gate.at[0], recv_gate.at[src])
    chunks = range(PLANE)
    decays = jnp.concatenate([gates[n, pl.ds(place, 1), :] for n in chunks], axis=0)
    rates = jnp.concatenate([gates[n, pl.ds(place + PLANE, 1), :] for n in chunks], axis=0)
    cum_rows, table = gate_tables(decays, rates)
    row, col = iotas()
    inclusive = row >= col
    cum_col = [jnp.broadcast_to(table[:, n : n + 1], (D, D)) for n in chunks]
    rate_col = [jnp.broadcast_to(table[:, PLANE + n : PLANE + n + 1], (D, D)) for n in chunks]
    within = []
    for n in chunks:
        spread = cum_col[n] - cum_rows[n : n + 1]
        within.append(jnp.where(inclusive, jnp.exp(jnp.where(inclusive, spread, 0.0)), 0.0))
    growth = [jnp.exp(cum_col[n]) for n in chunks]
    tail = [jnp.exp(cum_col[n][D - 1 : D, :] - cum_rows[n : n + 1]) for n in chunks]
    for copy in small[2:]:
        copy.wait()

    raw_arrived(0)
    activate(0)
    keys = [act[0, n] for n in chunks]
    keys_t = [keys[n].T for n in chunks]
    keys_right = [right(keys_t[n]) for n in chunks]
    key_key = [product(left(keys[n]), keys_right[n]) for n in chunks]
    systems = [jnp.where(row > col, rate_col[n] * within[n] * key_key[n], 0.0) for n in chunks]
    inverse = [left(x) for x in inverses(systems)]
    weighted = [left(keys_t[n] * tail[n]) for n in chunks]

    raw_arrived(1)
    activate(1)
    targets = [
        right(jnp.concatenate([(rate_col[n] * growth[n]) * keys[n], rate_col[n] * act[1, n]], axis=1)) for n in chunks
    ]
    solved = [right(product(inverse[n], targets[n])) for n in chunks]
    sign = jnp.concatenate([jnp.full((1, D), -1.0, F32), jnp.ones((1, D), F32)], axis=1)
    maps = [(growth[n][D - 1 : D, :], sign * product(weighted[n], solved[n])) for n in chunks]

    two = [compose(maps[n + 1], maps[n]) for n in range(0, PLANE, 2)]
    four = [compose(two[n + 1], two[n]) for n in range(0, PLANE // 2, 2)]
    total = compose(four[1], four[0])

    row16, _ = iotas(16)

    def put(slot, stretch, distance):
        d, both = stretch
        mine[slot, 0:D, :] = both.astype(BF16)
        high, rest = split(d)
        mid, low = split(d - high.astype(F32))
        digits = jnp.where(row16 == 0, high.astype(F32), jnp.where(row16 == 1, mid.astype(F32), low.astype(F32)))
        mine[slot, D : D + 16, 0:D] = jnp.where(row16 < 3, digits, 0.0).astype(BF16)
        mine[slot, D : D + 16, D : 2 * D] = jnp.zeros((16, D), BF16)
        send(mine.at[slot], got.at[slot], send_z.at[slot], recv_z.at[slot], (plane_at(distance) + place, head))

    def take(slot, distance):
        arrived(got.at[slot], send_z.at[slot], recv_z.at[slot])
        held = jnp.where(plane >= distance, got[slot].astype(F32), 0.0)
        return jnp.sum(held[D : D + 16, 0:D], axis=0, keepdims=True), held[0:D]

    put(0, total, 1)

    raw_arrived(2)
    activate(2)
    queries = [act[2, n] for n in chunks]
    scores = [left(within[n] * product(left(queries[n]), keys_right[n])) for n in chunks]
    seen = [product(scores[n], solved[n]) for n in chunks]
    response = [growth[n] * queries[n] - seen[n][:, :D] for n in chunks]
    prefix = {1: maps[0], 2: two[0], 4: four[0]}
    prefix[3] = compose(maps[2], two[0])
    prefix[5] = compose(maps[4], four[0])
    prefix[6] = compose(two[2], four[0])
    reach[0] = left(response[0])
    direct[0] = seen[0][:, D:]

    def reach_of(n):
        through = product(left(response[n]), right(prefix[n][1]))
        reach[n] = left(through[:, :D] + prefix[n][0] * response[n])
        direct[n] = through[:, D:] + seen[n][:, D:]

    one = take(0, 1)
    pair = compose(total, one)
    put(1, pair, 2)
    prefix[7] = compose(maps[6], prefix[6])
    for n in range(1, PLANE):
        reach_of(n)
    raw_arrived(3)
    for n in chunks:
        own[n] = silu(raw[3, n].astype(F32)) * gain[...]

    before = take(1, 2)
    mine[2, 0:D, 0:D] = compose(pair, before)[1][:, D:].astype(BF16)
    send(
        mine.at[2, 0:D, 0:D], got.at[2, 0:D, 0:D], send_z.at[2], recv_z.at[2], (plane_at(4) + place, head)
    )
    three = compose(one, before)
    arrived(got.at[2, 0:D, 0:D], send_z.at[2], recv_z.at[2])
    far = jnp.where(plane >= 4, got[2, 0:D, 0:D].astype(F32), 0.0)
    state = product(left(three[1][:, :D]), right(far)) + three[0] * far + three[1][:, D:]
    state = right(state)

    lanes = pl.ds(pl.multiple_of(place * D, D), D)
    halves = [slice(0, D // 2), slice(D // 2, D)]
    for h, rows in enumerate(halves):
        for n in chunks:
            heads_out = product(reach[n, rows, :], state) + direct[n, rows, :]
            scale = lax.rsqrt(jnp.mean(heads_out * heads_out, axis=-1, keepdims=True) + 1e-06)
            back[n, rows, :] = (heads_out * scale * own[n, rows, :]).astype(BF16)
        for r in range(1, PLANE):
            dest = peer(r)
            send(
                back.at[dest, rows, :], whole.at[rows, lanes],
                send_back.at[h, r - 1], recv_back.at[h, place], (first + dest, head),
            )
    whole[:, lanes] = back[place]
    w_copy.wait()

    width = out_ref.shape[1]
    for h, rows in enumerate(halves):
        for r in range(1, PLANE):
            src = peer(r)
            arrived(
                whole.at[rows, pl.ds(pl.multiple_of(src * D, D), D)], send_back.at[h, 0], recv_back.at[h, src]
            )
        for r in (2, 1, 3):
            dest = lax.rem(head + r, HEADS_X)
            weights = w_all[:, pl.ds(pl.multiple_of(dest * width, width), width)]
            x_send[r - 1, rows, :] = jnp.dot(whole[rows, :], weights, preferred_element_type=F32).astype(BF16)
            send(
                x_send.at[r - 1, rows, :], x_got.at[r - 1, rows, :],
                send_x.at[h, r - 1], recv_x.at[h, r - 1], (me, dest),
            )
    weights = w_all[:, pl.ds(pl.multiple_of(head * width, width), width)]
    share = jnp.dot(whole[...], weights, preferred_element_type=F32)
    for h, rows in enumerate(halves):
        part = share[rows]
        for r in (1, 3, 2):
            arrived(x_got.at[r - 1, rows, :], send_x.at[h, r - 1], recv_x.at[h, r - 1])
            part = part + x_got[r - 1, rows, :].astype(F32)
        out_ref[rows, :] = part.astype(BF16)
    for copy in sent:
        copy.wait_send()

    @pl.when(last)
    def _():
        for a in range(3):
            for j in range(PLANE):
                halo_copy(a, j).wait_send()


def on_device(q_in, k_in, v_in, z_gate, decay, rate, conv_q, conv_k, conv_v, norm_gain, w_out):
    tok, width = q_in.shape
    dma = pltpu.SemaphoreType.DMA
    return pl.pallas_call(
        kernel,
        out_shape=jax.ShapeDtypeStruct((tok, width), BF16),
        in_specs=[pl.BlockSpec(memory_space=pltpu.HBM)] * 11,
        out_specs=pl.BlockSpec(memory_space=VMEM),
        scratch_shapes=[
            VMEM((4, PLANE, D, D), BF16),
            VMEM((2 * PLANE, D), F32),
            VMEM((PLANE, 2 * PLANE, D), F32),
            VMEM((3, 16, D), BF16),
            VMEM((3, PLANE * D + 8, D), F32),
            VMEM((3, PLANE, D, D), F32),
            VMEM((3, 4, D), F32),
            VMEM((1, D), F32),
            VMEM((PLANE, D, 2 * D), BF16),
            VMEM((PLANE, D, D), F32),
            VMEM((3, D + 16, 2 * D), BF16),
            VMEM((3, D + 16, 2 * D), BF16),
            VMEM((PLANE, D, D), F32),
            VMEM((PLANE, D, D), BF16),
            VMEM((tok, PLANE * D), BF16),
            VMEM(w_out.shape, BF16),
            VMEM((HEADS_X - 1, tok, width), BF16),
            VMEM((HEADS_X - 1, tok, width), BF16),
            dma((4, PLANE - 1)), dma((4, PLANE)),
            dma((PLANE - 1,)), dma((PLANE,)),
            dma((3, PLANE)), dma((3,)),
            dma((3,)), dma((3,)),
            dma((2, PLANE - 1)), dma((2, PLANE)),
            dma((2, HEADS_X - 1)), dma((2, HEADS_X - 1)),
            dma, dma((6,)),
        ],
        compiler_params=pltpu.CompilerParams(
            collective_id=0, has_side_effects=True, vmem_limit_bytes=48 * 1024 * 1024
        ),
    )(q_in, k_in, v_in, z_gate, decay.T, rate.T, conv_q, conv_k, conv_v, norm_gain.reshape(1, D), w_out)


def solution(mesh):
    return jax.shard_map(
        on_device,
        mesh=mesh,
        in_specs=(
            P("seq", "head"),
            P("seq", "head"),
            P("seq", "head"),
            P("seq", "head"),
            P("seq", "head"),
            P("seq", "head"),
            P(None, "head"),
            P(None, "head"),
            P(None, "head"),
            P(),
            P("head", None),
        ),
        out_specs=P("seq", "head"),
        check_vma=False,
    )
```

time: 88.8 us -> 62.8 us (0.71)
  Pallas kernels: 78.2 us -> 51.7 us
  local copies, waits for them, and re-layouts: 9.47 us -> 10.7 us
    pallas_call x1, Pallas kernels: 78.2 us -> 51.7 us  [on_device(): pl.pallas_call(kernel, out_shape=jax.ShapeDtypeStruct((tok, width), BF16)...]
    unnamed x19 -> x23, local copies, waits for them, and re-layouts: 9.32 us -> 10.7 us
where the time goes in v2:
time: 62.8 us; the launch traced here: 62.4 us
  Pallas kernels  51.7 us (82%)
  local copies, waits for them, and re-layouts  10.7 us (17%)
    pallas_call x1, Pallas kernels, on_device(): pl.pallas_call(kernel, out_shape=jax.ShapeDtypeStruct((tok, width), BF16)...  51.7 us
    unnamed x23, local copies, waits for them, and re-layouts  10.7 us

profile of v2, /device:TPU:1, one launch (start us, length us, event | category | flops | bytes accessed | tf_op | source)
XLA Modules:
  0.0 62.4 jit_solution(11842289357332306694)
XLA Ops:
  0.0 0.0 copy-start
  0.0 2.2 %copy-done = bf16[1024,2048]{1,0:T(8,128)(2,1)S(1)} copy-done((bf16[1024,2048]{1,0:T(8,128)(2,1)S(1)}, bf16[1024,2048]{1,0:T(8,128)(2,1)}, u32[]{:S(2)}) %copy-start) | copy-done | bytes 4194328
  2.2 0.0 copy-start.1
  2.2 0.9 %copy-done.1 = bf16[128,1024]{1,0:T(8,128)(2,1)S(1)} copy-done((bf16[128,1024]{1,0:T(8,128)(2,1)S(1)}, bf16[128,1024]{1,0:T(8,128)(2,1)}, u32[]{:S(2)}) %copy-start.1) | copy-done | bytes 262168
  3.1 0.0 copy-start.2
  3.1 0.9 %copy-done.2 = bf16[128,1024]{1,0:T(8,128)(2,1)S(1)} copy-done((bf16[128,1024]{1,0:T(8,128)(2,1)S(1)}, bf16[128,1024]{1,0:T(8,128)(2,1)}, u32[]{:S(2)}) %copy-start.2) | copy-done | bytes 262168
  4.1 0.0 copy-start.3
  4.1 0.9 %copy-done.3 = bf16[128,512]{1,0:T(8,128)(2,1)S(1)} copy-done((bf16[128,512]{1,0:T(8,128)(2,1)S(1)}, bf16[128,512]{1,0:T(8,128)(2,1)}, u32[]{:S(2)}) %copy-start.3) | copy-done | bytes 131096
  5.0 0.0 copy-start.4
  5.0 0.9 %copy-done.4 = bf16[128,512]{1,0:T(8,128)(2,1)S(1)} copy-done((bf16[128,512]{1,0:T(8,128)(2,1)S(1)}, bf16[128,512]{1,0:T(8,128)(2,1)}, u32[]{:S(2)}) %copy-start.4) | copy-done | bytes 131096
  5.9 0.0 copy-start.5
  5.9 0.7 %copy-done.5 = f32[4,1024]{1,0:T(4,128)S(1)} copy-done((f32[4,1024]{1,0:T(4,128)S(1)}, f32[4,1024]{1,0:T(4,128)}, u32[]{:S(2)}) %copy-start.5) | copy-done | bytes 16408
  6.6 0.0 copy-start.6
  6.6 0.7 %copy-done.6 = f32[4,512]{1,0:T(4,128)S(1)} copy-done((f32[4,512]{1,0:T(4,128)S(1)}, f32[4,512]{1,0:T(4,128)}, u32[]{:S(2)}) %copy-start.6) | copy-done | bytes 8216
  7.3 0.0 copy-start.7
  7.3 0.7 %copy-done.7 = f32[4,512]{1,0:T(4,128)S(1)} copy-done((f32[4,512]{1,0:T(4,128)S(1)}, f32[4,512]{1,0:T(4,128)}, u32[]{:S(2)}) %copy-start.7) | copy-done | bytes 8216
  8.0 0.0 copy-start.8
  8.0 0.7 %copy-done.8 = f32[128,8]{0,1:T(8,128)S(1)} copy-done((f32[128,8]{0,1:T(8,128)S(1)}, f32[128,8]{0,1:T(8,128)}, u32[]{:S(2)}) %copy-start.8) | copy-done | bytes 4120
  8.7 0.0 copy-start.9
  8.7 0.7 %copy-done.9 = f32[128,8]{0,1:T(8,128)S(1)} copy-done((f32[128,8]{0,1:T(8,128)S(1)}, f32[128,8]{0,1:T(8,128)}, u32[]{:S(2)}) %copy-start.9) | copy-done | bytes 4120
  9.4 0.0 copy-start.10
  9.4 0.7 %copy-done.10 = f32[128]{0:T(128)S(1)} copy-done((f32[128]{0:T(128)S(1)}, f32[128]{0:T(128)}, u32[]{:S(2)}) %copy-start.10) | copy-done | bytes 536
  10.0 51.7 %shard_map.109 = bf16[128,512]{1,0:T(8,128)(2,1)S(1)} custom-call(bf16[128,512]{1,0:T(8,128)(2,1)S(1)} %copy-done.3, bf16[128,512]{1,0:T(8,128)(2,1)S(1)} %copy-done.4, bf16[128,1024]{1,0:T(8,128)(2,1)S(1)} %copy-done.1, bf16[128,1024]{1,0:T(8,128)(2,1)S(1)} %copy-done.2, f32[8,128]{1,0:T(8,128)S(1)} %bitcast.3, f32[8,128]{1,0:T(8,128)S(1)} %bitcast.4, ...), custom_call_target="tpu_custom_call" | custom-call | tf_op jit(solution)/shard_map/pallas_call | solution.py:381
  61.7 0.7 %copy.13 = bf16[128,512]{1,0:T(8,128)(2,1)} copy(bf16[128,512]{1,0:T(8,128)(2,1)S(1)} %shard_map.109) | data formatting | bytes 262144
Async XLA Ops:
  0.0 2.2 %copy-start = (bf16[1024,2048]{1,0:T(8,128)(2,1)S(1)}, bf16[1024,2048]{1,0:T(8,128)(2,1)}, u32[]{:S(2)}) copy-start(bf16[1024,2048]{1,0:T(8,128)(2,1)} %w_ref.1) | copy-start | bytes 12582916
  2.2 0.9 %copy-start.1 = (bf16[128,1024]{1,0:T(8,128)(2,1)S(1)}, bf16[128,1024]{1,0:T(8,128)(2,1)}, u32[]{:S(2)}) copy-start(bf16[128,1024]{1,0:T(8,128)(2,1)} %v_ref.1) | copy-start | bytes 786436
  3.1 0.9 %copy-start.2 = (bf16[128,1024]{1,0:T(8,128)(2,1)S(1)}, bf16[128,1024]{1,0:T(8,128)(2,1)}, u32[]{:S(2)}) copy-start(bf16[128,1024]{1,0:T(8,128)(2,1)} %z_ref.1) | copy-start | bytes 786436
  4.1 0.9 %copy-start.3 = (bf16[128,512]{1,0:T(8,128)(2,1)S(1)}, bf16[128,512]{1,0:T(8,128)(2,1)}, u32[]{:S(2)}) copy-start(bf16[128,512]{1,0:T(8,128)(2,1)} %q_ref.1) | copy-start | bytes 393220
  5.0 0.9 %copy-start.4 = (bf16[128,512]{1,0:T(8,128)(2,1)S(1)}, bf16[128,512]{1,0:T(8,128)(2,1)}, u32[]{:S(2)}) copy-start(bf16[128,512]{1,0:T(8,128)(2,1)} %k_ref.1) | copy-start | bytes 393220
  5.9 0.7 %copy-start.5 = (f32[4,1024]{1,0:T(4,128)S(1)}, f32[4,1024]{1,0:T(4,128)}, u32[]{:S(2)}) copy-start(f32[4,1024]{1,0:T(4,128)} %cv_ref.1) | copy-start | bytes 49156
  6.6 0.7 %copy-start.6 = (f32[4,512]{1,0:T(4,128)S(1)}, f32[4,512]{1,0:T(4,128)}, u32[]{:S(2)}) copy-start(f32[4,512]{1,0:T(4,128)} %cq_ref.1) | copy-start | bytes 24580
  7.3 0.7 %copy-start.7 = (f32[4,512]{1,0:T(4,128)S(1)}, f32[4,512]{1,0:T(4,128)}, u32[]{:S(2)}) copy-start(f32[4,512]{1,0:T(4,128)} %ck_ref.1) | copy-start | bytes 24580
  8.0 0.7 %copy-start.8 = (f32[128,8]{0,1:T(8,128)S(1)}, f32[128,8]{0,1:T(8,128)}, u32[]{:S(2)}) copy-start(f32[128,8]{0,1:T(8,128)} %param.15) | copy-start | bytes 12292
  8.7 0.7 %copy-start.9 = (f32[128,8]{0,1:T(8,128)S(1)}, f32[128,8]{0,1:T(8,128)}, u32[]{:S(2)}) copy-start(f32[128,8]{0,1:T(8,128)} %param.16) | copy-start | bytes 12292
  9.4 0.7 %copy-start.10 = (f32[128]{0:T(128)S(1)}, f32[128]{0:T(128)}, u32[]{:S(2)}) copy-start(f32[128]{0:T(128)} %param.20) | copy-start | bytes 1540

commit v3 on v2

--- a/solution.py
+++ b/solution.py
@@ -11,6 +11,7 @@
 PLANE = 8
 PLANES = 8
 HEADS_X = 4
+PIECES = 2
 MESH = pl.DeviceIdType.MESH
 VMEM = pltpu.VMEM
 
@@ -31,10 +32,11 @@
     return jnp.concatenate([both, both], axis=0)
 
 
-def product(lhs, rhs):
+def product(lhs, rhs, count=1):
     both = jnp.dot(lhs, rhs, preferred_element_type=F32)
-    half = both.shape[1] // 2
-    return both[:, :half] + both[:, half:]
+    half = both.shape[1] // (2 * count)
+    parts = [both[:, 2 * i * half : (2 * i + 1) * half] + both[:, (2 * i + 1) * half : (2 * i + 2) * half] for i in range(count)]
+    return parts[0] if count == 1 else jnp.concatenate(parts, axis=1)
 
 
 def silu(x):
@@ -90,20 +92,28 @@
     return result
 
 
-def compose(later, earlier):
-    d_later, both_later = later
-    d_earlier, both_earlier = earlier
-    joined = product(left(both_later[:, :D]), right(both_earlier))
-    wide = jnp.concatenate([d_later, d_later], axis=1)
-    factors = jnp.concatenate([d_earlier, jnp.ones_like(d_earlier)], axis=1)
-    return d_later * d_earlier, joined + wide * both_earlier + factors * both_later
+def product_once(linear, b):
+    whole = jnp.dot(linear[2], jnp.concatenate([b, b], axis=0), preferred_element_type=F32)
+    return whole + linear[0] * b.astype(F32)
+
+
+def join(later, earlier):
+    d_later, m_later, split_later = later
+    d_earlier, m_earlier, _ = earlier
+    m = product(split_later, right(m_earlier)) + d_later * m_earlier + d_earlier * m_later
+    return d_later * d_earlier, m, left(m)
+
+
+def advance(later, b_later, b_earlier):
+    return product(later[2], right(b_earlier)) + later[0] * b_earlier + b_later
 
 
 def kernel(
     q_ref, k_ref, v_ref, z_ref, decay_ref, rate_ref, cq_ref, ck_ref, cv_ref, gain_ref, w_ref, out_ref,
-    raw, gate_own, gates, halo, ext, act, taps, gain, reach, direct, mine, got, own, back, whole, w_all, x_send, x_got,
-    send_raw, recv_raw, send_gate, recv_gate, send_halo, recv_halo, send_z, recv_z,
-    send_back, recv_back, send_x, recv_x, w_sem, small_sem,
+    blocks, raw, gate_own, gate_tiles, gates, halo, ext, act, taps, gain, reach, direct,
+    mine_m, got_m, mine_b, got_b, own, back, whole, w_all, x_send, x_got,
+    send_raw, recv_raw, send_gate, recv_gate, send_halo, recv_halo, send_m, recv_m, send_b, recv_b,
+    send_back, recv_back, send_x, recv_x, w_sem, small_sem, block_sem, known,
 ):
     me, head = lax.axis_index("seq"), lax.axis_index("head")
     plane, place = me // PLANE, lax.rem(me, PLANE)
@@ -139,17 +149,30 @@
 
     barrier = pltpu.get_barrier_semaphore()
     near = [(first + peer(r), head) for r in range(1, PLANE)]
-    near += [(plane_at(r) + place, head) for r in (1, -1, 2, -2, 4)]
     near += [(me, lax.rem(head + r, HEADS_X)) for r in range(1, HEADS_X)]
     for device in near:
         pl.semaphore_signal(barrier, inc=1, device_id=device, device_id_type=MESH)
 
-    @pl.when(jnp.logical_not(last))
-    def _():
-        pl.semaphore_signal(barrier, inc=1, device_id=(plane_at(-1) + PLANE - 1, head), device_id_type=MESH)
-
+    def tell(sem, r):
+        pl.semaphore_signal(sem, inc=1, device_id=(plane_at(r) + place, head), device_id_type=MESH)
+
+    @pl.when(plane > 0)
+    def _():
+        tell(barrier, -1)
+
+        @pl.when(jnp.logical_not(last))
+        def _():
+            pl.semaphore_signal(barrier, inc=1, device_id=(plane_at(-1) + PLANE - 1, head), device_id_type=MESH)
+
+    local = []
     kept = []
     for a in range(4):
+        for b in range(PLANE if a % 2 else PLANE // 2):
+            copy = pltpu.make_async_copy(
+                sources[a].at[:, b * D : (b + 1) * D], blocks.at[a, b], block_sem.at[a, b]
+            )
+            copy.start()
+            local.append((a, copy))
         copy = pltpu.make_async_copy(
             sources[a].at[:, columns(a, place)], raw.at[a, place], recv_raw.at[a, place]
         )
@@ -159,8 +182,16 @@
     w_copy.start()
     for copy in small[:2]:
         copy.wait()
-
-    pl.semaphore_wait(barrier, len(near) + jnp.where(last, PLANE - 1, 0))
+    for j in range(PLANE):
+        gate_tiles[j] = jnp.concatenate(
+            [gate_own[j : j + 1, :], gate_own[PLANE + j : PLANE + j + 1, :], jnp.zeros((6, D), F32)], axis=0
+        )
+    for a, copy in local:
+        if a < 2:
+            copy.wait()
+
+    after = plane < PLANES - 1
+    pl.semaphore_wait(barrier, len(near) + jnp.where(after, 1 + jnp.where(last, PLANE - 1, 0), 0))
 
     sent = []
 
@@ -179,26 +210,32 @@
 
     def halo_copy(a, j):
         return remote(
-            sources[a].at[D - 16 : D, columns(a, j)], halo.at[a],
+            blocks.at[a, j if a % 2 else j // 2, D - 16 : D, :], halo.at[a],
             send_halo.at[a, j], recv_halo.at[a], (plane_at(1) + j, head),
         )
 
-    for r in range(1, PLANE):
-        dest = peer(r)
-        send(gate_own, gates.at[place], send_gate.at[r - 1], recv_gate.at[place], (first + dest, head))
-    for a in range(4):
+    def raw_send(a):
         for r in range(1, PLANE):
             dest = peer(r)
             send(
-                sources[a].at[:, columns(a, dest)], raw.at[a, place],
+                blocks.at[a, dest if a % 2 else dest // 2], raw.at[a, place],
                 send_raw.at[a, r - 1], recv_raw.at[a, place], (first + dest, head),
             )
         if a < 3:
 
-            @pl.when(last)
+            @pl.when(jnp.logical_and(last, after))
             def _():
                 for j in range(PLANE):
                     halo_copy(a, j).start()
+
+    raw_send(0)
+    for r in range(1, PLANE):
+        dest = peer(r)
+        send(gate_tiles.at[dest], gates.at[place], send_gate.at[r - 1], recv_gate.at[place], (first + dest, head))
+    raw_send(1)
+    for a, copy in local:
+        if a >= 2:
+            copy.wait()
 
     def raw_arrived(a):
         kept[a].wait()
@@ -206,11 +243,13 @@
             src = peer(r)
             arrived(raw.at[a, src], send_raw.at[a, 0], recv_raw.at[a, src])
         if a < 3:
-            arrived(halo.at[a], send_halo.at[a, 0], recv_halo.at[a])
+
+            @pl.when(plane > 0)
+            def _():
+                arrived(halo.at[a], send_halo.at[a, 0], recv_halo.at[a])
 
     def activate(a):
-        before = jnp.where(plane > 0, halo[a].astype(F32), 0.0)
-        ext[a, 0:8, :] = before[8:16]
+        ext[a, 0:8, :] = jnp.where(plane > 0, halo[a].astype(F32), 0.0)[8:16]
         for n in range(PLANE):
             ext[a, 8 + n * D : 8 + (n + 1) * D, :] = raw[a, n].astype(F32)
         for n in range(PLANE):
@@ -224,13 +263,13 @@
                 total = total * D ** (-0.5)
             act[a, n] = total
 
-    gates[place] = gate_own[...]
+    gates[place] = gate_tiles[place]
     for r in range(1, PLANE):
         src = peer(r)
         arrived(gates.at[src], send_gate.at[0], recv_gate.at[src])
     chunks = range(PLANE)
-    decays = jnp.concatenate([gates[n, pl.ds(place, 1), :] for n in chunks], axis=0)
-    rates = jnp.concatenate([gates[n, pl.ds(place + PLANE, 1), :] for n in chunks], axis=0)
+    decays = jnp.concatenate([gates[n, 0:1, :] for n in chunks], axis=0)
+    rates = jnp.concatenate([gates[n, 1:2, :] for n in chunks], axis=0)
     cum_rows, table = gate_tables(decays, rates)
     row, col = iotas()
     inclusive = row >= col
@@ -246,6 +285,13 @@
         copy.wait()
 
     raw_arrived(0)
+
+    @pl.when(jnp.logical_and(plane > 0, after))
+    def _():
+        tell(known.at[0], -1)
+        tell(known.at[1], 1)
+
+    raw_send(2)
     activate(0)
     keys = [act[0, n] for n in chunks]
     keys_t = [keys[n].T for n in chunks]
@@ -254,80 +300,149 @@
     systems = [jnp.where(row > col, rate_col[n] * within[n] * key_key[n], 0.0) for n in chunks]
     inverse = [left(x) for x in inverses(systems)]
     weighted = [left(keys_t[n] * tail[n]) for n in chunks]
-
-    raw_arrived(1)
-    activate(1)
-    targets = [
-        right(jnp.concatenate([(rate_col[n] * growth[n]) * keys[n], rate_col[n] * act[1, n]], axis=1)) for n in chunks
-    ]
-    solved = [right(product(inverse[n], targets[n])) for n in chunks]
-    sign = jnp.concatenate([jnp.full((1, D), -1.0, F32), jnp.ones((1, D), F32)], axis=1)
-    maps = [(growth[n][D - 1 : D, :], sign * product(weighted[n], solved[n])) for n in chunks]
-
-    two = [compose(maps[n + 1], maps[n]) for n in range(0, PLANE, 2)]
-    four = [compose(two[n + 1], two[n]) for n in range(0, PLANE // 2, 2)]
-    total = compose(four[1], four[0])
+    solved_k = [right(product(inverse[n], right((rate_col[n] * growth[n]) * keys[n]))) for n in chunks]
+    maps = []
+    for n in chunks:
+        m = -product(weighted[n], solved_k[n])
+        maps.append((growth[n][D - 1 : D, :], m, left(m)))
+    two = [join(maps[n + 1], maps[n]) for n in range(0, PLANE, 2)]
+    four = [join(two[n + 1], two[n]) for n in range(0, PLANE // 2, 2)]
+    total = join(four[1], four[0])
 
     row16, _ = iotas(16)
 
-    def put(slot, stretch, distance):
-        d, both = stretch
-        mine[slot, 0:D, :] = both.astype(BF16)
+    def put_m(slot, linear):
+        d, m, _ = linear
+        mine_m[slot, 0:D, :] = m.astype(BF16)
         high, rest = split(d)
         mid, low = split(d - high.astype(F32))
         digits = jnp.where(row16 == 0, high.astype(F32), jnp.where(row16 == 1, mid.astype(F32), low.astype(F32)))
-        mine[slot, D : D + 16, 0:D] = jnp.where(row16 < 3, digits, 0.0).astype(BF16)
-        mine[slot, D : D + 16, D : 2 * D] = jnp.zeros((16, D), BF16)
-        send(mine.at[slot], got.at[slot], send_z.at[slot], recv_z.at[slot], (plane_at(distance) + place, head))
-
-    def take(slot, distance):
-        arrived(got.at[slot], send_z.at[slot], recv_z.at[slot])
-        held = jnp.where(plane >= distance, got[slot].astype(F32), 0.0)
-        return jnp.sum(held[D : D + 16, 0:D], axis=0, keepdims=True), held[0:D]
-
-    put(0, total, 1)
+        mine_m[slot, D : D + 16, :] = jnp.where(row16 < 3, digits, 0.0).astype(BF16)
+
+    def m_copy(src, dst, r):
+        return remote(mine_m.at[src], got_m.at[dst], send_m.at[dst], recv_m.at[dst], (plane_at(r) + place, head))
+
+    def b_copy(src, dst, r):
+        return remote(mine_b.at[src], got_b.at[dst], send_b.at[dst], recv_b.at[dst], (plane_at(r) + place, head))
+
+    hops = {
+        "m1": (m_copy(0, 0, 1), 1, 6),
+        "m2": (m_copy(1, 1, 2), 2, 5),
+        "m4": (m_copy(1, 2, 4), 2, 3),
+        "b1": (b_copy(0, 0, 1), 0, 6),
+        "b2": (b_copy(1, 1, 2), 0, 5),
+        "b4": (b_copy(1, 2, 4), 0, 3),
+        "b6": (b_copy(1, 3, 6), 0, 1),
+    }
+
+    def hop(name, act_on):
+        copy, low, high = hops[name]
+        distance = int(name[1])
+        shift = 0 if act_on != "wait_recv" else distance
+
+        @pl.when(jnp.logical_and(plane >= low + shift, plane <= high + shift))
+        def _():
+            getattr(copy, act_on)()
+
+    def take_m(slot, name):
+        hop(name, "wait_recv")
+        held = jnp.where(plane >= hops[name][1] + int(name[1]), got_m[slot].astype(F32), 0.0)
+        return jnp.sum(held[D : D + 16], axis=0, keepdims=True), held[0:D], left(held[0:D])
+
+    def take_b(slot, name):
+        hop(name, "wait_recv")
+        return jnp.where(plane >= int(name[1]), got_b[slot].astype(F32), 0.0).astype(BF16)
+
+    put_m(0, total)
+    hop("m1", "start")
+
+    raw_arrived(1)
+    raw_send(3)
+    activate(1)
+    solved_v = [right(product(inverse[n], right(rate_col[n] * act[1, n]))) for n in chunks]
+    offsets = [product(weighted[n], solved_v[n]) for n in chunks]
+    two_b = [advance(maps[n + 1], offsets[n + 1], offsets[n]) for n in range(0, PLANE, 2)]
+    four_b = [advance(two[n + 1], two_b[n + 1], two_b[n]) for n in range(0, PLANE // 2, 2)]
+    total_b = advance(four[1], four_b[1], four_b[0])
+    mine_b[0] = total_b.astype(BF16)
+    hop("b1", "start")
+
+    @pl.when(plane <= 5)
+    def _():
+        pl.semaphore_wait(known.at[0], 1)
+
+    @pl.when(plane >= 2)
+    def _():
+        pl.semaphore_wait(known.at[1], 1)
+
+    @pl.when(jnp.logical_and(plane >= 2, plane <= 5))
+    def _():
+        tell(known.at[2], -2)
 
     raw_arrived(2)
     activate(2)
     queries = [act[2, n] for n in chunks]
     scores = [left(within[n] * product(left(queries[n]), keys_right[n])) for n in chunks]
-    seen = [product(scores[n], solved[n]) for n in chunks]
-    response = [growth[n] * queries[n] - seen[n][:, :D] for n in chunks]
+    response = [growth[n] * queries[n] - product(scores[n], solved_k[n]) for n in chunks]
+    seen = [product(scores[n], solved_v[n]) for n in chunks]
+
+    one = take_m(0, "m1")
+    pair = join(total, one)
+    put_m(1, pair)
+
+    @pl.when(plane <= 3)
+    def _():
+        pl.semaphore_wait(known.at[2], 1)
+
+    @pl.when(jnp.logical_and(plane >= 2, plane <= 3))
+    def _():
+        tell(known.at[3], -2)
+
+    hop("m4", "start")
+    hop("m2", "start")
+    one_b = take_b(0, "b1")
+    pair_b = product_once(total, one_b) + total_b
+    mine_b[1] = pair_b.astype(BF16)
+    hop("b4", "start")
+    hop("b2", "start")
+
+    @pl.when(plane <= 1)
+    def _():
+        pl.semaphore_wait(known.at[3], 1)
+
+    hop("b6", "start")
+
     prefix = {1: maps[0], 2: two[0], 4: four[0]}
-    prefix[3] = compose(maps[2], two[0])
-    prefix[5] = compose(maps[4], four[0])
-    prefix[6] = compose(two[2], four[0])
+    prefix_b = {1: offsets[0], 2: two_b[0], 4: four_b[0]}
+    for n, later, later_b, earlier in (
+        (3, maps[2], offsets[2], 2),
+        (5, maps[4], offsets[4], 4),
+        (6, two[2], two_b[2], 4),
+        (7, maps[6], offsets[6], 6),
+    ):
+        prefix[n] = join(later, prefix[earlier])
+        prefix_b[n] = advance(later, later_b, prefix_b[earlier])
     reach[0] = left(response[0])
-    direct[0] = seen[0][:, D:]
-
-    def reach_of(n):
-        through = product(left(response[n]), right(prefix[n][1]))
+    direct[0] = seen[0]
+    for n in range(1, PLANE):
+        through = product(
+            left(response[n]), jnp.concatenate([right(prefix[n][1]), right(prefix_b[n])], axis=1), 2
+        )
         reach[n] = left(through[:, :D] + prefix[n][0] * response[n])
-        direct[n] = through[:, D:] + seen[n][:, D:]
-
-    one = take(0, 1)
-    pair = compose(total, one)
-    put(1, pair, 2)
-    prefix[7] = compose(maps[6], prefix[6])
-    for n in range(1, PLANE):
-        reach_of(n)
+        direct[n] = through[:, D:] + seen[n]
     raw_arrived(3)
     for n in chunks:
         own[n] = silu(raw[3, n].astype(F32)) * gain[...]
 
-    before = take(1, 2)
-    mine[2, 0:D, 0:D] = compose(pair, before)[1][:, D:].astype(BF16)
-    send(
-        mine.at[2, 0:D, 0:D], got.at[2, 0:D, 0:D], send_z.at[2], recv_z.at[2], (plane_at(4) + place, head)
-    )
-    three = compose(one, before)
-    arrived(got.at[2, 0:D, 0:D], send_z.at[2], recv_z.at[2])
-    far = jnp.where(plane >= 4, got[2, 0:D, 0:D].astype(F32), 0.0)
-    state = product(left(three[1][:, :D]), right(far)) + three[0] * far + three[1][:, D:]
+    two_back = join(one, take_m(1, "m2"))
+    four_back = join(two_back, take_m(2, "m4"))
+    state = one_b.astype(F32)
+    for linear, slot, name in ((one, 1, "b2"), (two_back, 2, "b4"), (four_back, 3, "b6")):
+        state = state + product_once(linear, take_b(slot, name))
     state = right(state)
 
     lanes = pl.ds(pl.multiple_of(place * D, D), D)
-    halves = [slice(0, D // 2), slice(D // 2, D)]
+    halves = [slice(h * D // PIECES, (h + 1) * D // PIECES) for h in range(PIECES)]
     for h, rows in enumerate(halves):
         for n in chunks:
             heads_out = product(reach[n, rows, :], state) + direct[n, rows, :]
@@ -368,7 +483,10 @@
     for copy in sent:
         copy.wait_send()
 
-    @pl.when(last)
+    for name in hops:
+        hop(name, "wait_send")
+
+    @pl.when(jnp.logical_and(last, after))
     def _():
         for a in range(3):
             for j in range(PLANE):
@@ -385,8 +503,10 @@
         out_specs=pl.BlockSpec(memory_space=VMEM),
         scratch_shapes=[
             VMEM((4, PLANE, D, D), BF16),
+            VMEM((4, PLANE, D, D), BF16),
             VMEM((2 * PLANE, D), F32),
-            VMEM((PLANE, 2 * PLANE, D), F32),
+            VMEM((PLANE, 8, D), F32),
+            VMEM((PLANE, 8, D), F32),
             VMEM((3, 16, D), BF16),
             VMEM((3, PLANE * D + 8, D), F32),
             VMEM((3, PLANE, D, D), F32),
@@ -394,8 +514,10 @@
             VMEM((1, D), F32),
             VMEM((PLANE, D, 2 * D), BF16),
             VMEM((PLANE, D, D), F32),
-            VMEM((3, D + 16, 2 * D), BF16),
-            VMEM((3, D + 16, 2 * D), BF16),
+            VMEM((2, D + 16, D), BF16),
+            VMEM((3, D + 16, D), BF16),
+            VMEM((2, D, D), BF16),
+            VMEM((4, D, D), BF16),
             VMEM((PLANE, D, D), F32),
             VMEM((PLANE, D, D), BF16),
             VMEM((tok, PLANE * D), BF16),
@@ -406,12 +528,14 @@
             dma((PLANE - 1,)), dma((PLANE,)),
             dma((3, PLANE)), dma((3,)),
             dma((3,)), dma((3,)),
-            dma((2, PLANE - 1)), dma((2, PLANE)),
-            dma((2, HEADS_X - 1)), dma((2, HEADS_X - 1)),
-            dma, dma((6,)),
+            dma((4,)), dma((4,)),
+            dma((PIECES, PLANE - 1)), dma((PIECES, PLANE)),
+            dma((PIECES, HEADS_X - 1)), dma((PIECES, HEADS_X - 1)),
+            dma, dma((6,)), dma((4, PLANE)),
+            pltpu.SemaphoreType.REGULAR((4,)),
         ],
         compiler_params=pltpu.CompilerParams(
-            collective_id=0, has_side_effects=True, vmem_limit_bytes=48 * 1024 * 1024
+            collective_id=0, has_side_effects=True, vmem_limit_bytes=60 * 1024 * 1024
         ),
     )(q_in, k_in, v_in, z_gate, decay.T, rate.T, conv_q, conv_k, conv_v, norm_gain.reshape(1, D), w_out)
 

time: 62.8 us -> 44.3 us (0.71)
  the two profiles are of different devices: /device:TPU:1 before, /device:TPU:161 now
where the time goes in v3:
time: 44.3 us; the launch traced here: 44.2 us
  Pallas kernels  42.7 us (96%)
  local copies, waits for them, and re-layouts  1.57 us (4%)
    pallas_call x1, Pallas kernels, on_device(): pl.pallas_call(kernel, out_shape=jax.ShapeDtypeStruct((tok, width), BF16)...  42.7 us
    unnamed x1, local copies, waits for them, and re-layouts  1.57 us

profile of v3, /device:TPU:161, one launch (start us, length us, event | category | flops | bytes accessed | tf_op | source)
XLA Modules:
  0.0 44.2 jit_solution(4350378228711374231)
XLA Ops:
  0.0 42.7 %shard_map.109 = bf16[128,512]{1,0:T(8,128)(2,1)} custom-call(bf16[128,512]{1,0:T(8,128)(2,1)} %q_ref.1, bf16[128,512]{1,0:T(8,128)(2,1)} %k_ref.1, bf16[128,1024]{1,0:T(8,128)(2,1)} %v_ref.1, bf16[128,1024]{1,0:T(8,128)(2,1)} %z_ref.1, f32[8,128]{1,0:T(8,128)} %bitcast.3, f32[8,128]{1,0:T(8,128)} %bitcast.4, f32[4,512]{1,0:T(4,128)} %cq_ref.1, ...), custom_call_target="tpu_custom_call" | custom-call | tf_op jit(solution)/shard_map/pallas_call | solution.py:499
  42.7 1.6 %copy.13 = bf16[128,512]{1,0:T(8,128)(2,1)} copy(bf16[128,512]{1,0:T(8,128)(2,1)} %shard_map.109) | data formatting | bytes 262144

commit v4 on v3

--- a/solution.py
+++ b/solution.py
@@ -11,7 +11,7 @@
 PLANE = 8
 PLANES = 8
 HEADS_X = 4
-PIECES = 2
+PIECES = 4
 MESH = pl.DeviceIdType.MESH
 VMEM = pltpu.VMEM
 
@@ -156,13 +156,11 @@
     def tell(sem, r):
         pl.semaphore_signal(sem, inc=1, device_id=(plane_at(r) + place, head), device_id_type=MESH)
 
-    @pl.when(plane > 0)
-    def _():
-        tell(barrier, -1)
-
-        @pl.when(jnp.logical_not(last))
-        def _():
-            pl.semaphore_signal(barrier, inc=1, device_id=(plane_at(-1) + PLANE - 1, head), device_id_type=MESH)
+    tell(barrier, -1)
+
+    @pl.when(jnp.logical_and(plane > 0, jnp.logical_not(last)))
+    def _():
+        pl.semaphore_signal(barrier, inc=1, device_id=(plane_at(-1) + PLANE - 1, head), device_id_type=MESH)
 
     local = []
     kept = []
@@ -191,7 +189,7 @@
             copy.wait()
 
     after = plane < PLANES - 1
-    pl.semaphore_wait(barrier, len(near) + jnp.where(after, 1 + jnp.where(last, PLANE - 1, 0), 0))
+    pl.semaphore_wait(barrier, len(near) + 1 + jnp.where(jnp.logical_and(last, after), PLANE - 1, 0))
 
     sent = []
 
@@ -228,14 +226,21 @@
                 for j in range(PLANE):
                     halo_copy(a, j).start()
 
-    raw_send(0)
     for r in range(1, PLANE):
         dest = peer(r)
         send(gate_tiles.at[dest], gates.at[place], send_gate.at[r - 1], recv_gate.at[place], (first + dest, head))
+    raw_send(0)
     raw_send(1)
+
+    @pl.when(plane == PLANES - 1)
+    def _():
+        tell(known.at[4], 1)
+
     for a, copy in local:
         if a >= 2:
             copy.wait()
+    raw_send(2)
+    raw_send(3)
 
     def raw_arrived(a):
         kept[a].wait()
@@ -291,7 +296,15 @@
         tell(known.at[0], -1)
         tell(known.at[1], 1)
 
-    raw_send(2)
+    @pl.when(plane == PLANES - 1)
+    def _():
+        tell(known.at[3], 1)
+
+    @pl.when(plane == 0)
+    def _():
+        pl.semaphore_wait(known.at[4], 1)
+        tell(known.at[3], 1)
+
     activate(0)
     keys = [act[0, n] for n in chunks]
     keys_t = [keys[n].T for n in chunks]
@@ -300,6 +313,18 @@
     systems = [jnp.where(row > col, rate_col[n] * within[n] * key_key[n], 0.0) for n in chunks]
     inverse = [left(x) for x in inverses(systems)]
     weighted = [left(keys_t[n] * tail[n]) for n in chunks]
+    @pl.when(plane <= 5)
+    def _():
+        pl.semaphore_wait(known.at[0], 1)
+
+    @pl.when(plane >= 2)
+    def _():
+        pl.semaphore_wait(known.at[1], 1)
+
+    @pl.when(jnp.logical_and(plane >= 2, plane <= 5))
+    def _():
+        tell(known.at[2], -2)
+
     solved_k = [right(product(inverse[n], right((rate_col[n] * growth[n]) * keys[n]))) for n in chunks]
     maps = []
     for n in chunks:
@@ -357,7 +382,6 @@
     hop("m1", "start")
 
     raw_arrived(1)
-    raw_send(3)
     activate(1)
     solved_v = [right(product(inverse[n], right(rate_col[n] * act[1, n]))) for n in chunks]
     offsets = [product(weighted[n], solved_v[n]) for n in chunks]
@@ -367,18 +391,6 @@
     mine_b[0] = total_b.astype(BF16)
     hop("b1", "start")
 
-    @pl.when(plane <= 5)
-    def _():
-        pl.semaphore_wait(known.at[0], 1)
-
-    @pl.when(plane >= 2)
-    def _():
-        pl.semaphore_wait(known.at[1], 1)
-
-    @pl.when(jnp.logical_and(plane >= 2, plane <= 5))
-    def _():
-        tell(known.at[2], -2)
-
     raw_arrived(2)
     activate(2)
     queries = [act[2, n] for n in chunks]
@@ -394,17 +406,13 @@
     def _():
         pl.semaphore_wait(known.at[2], 1)
 
-    @pl.when(jnp.logical_and(plane >= 2, plane <= 3))
-    def _():
-        tell(known.at[3], -2)
-
+    hop("m2", "start")
     hop("m4", "start")
-    hop("m2", "start")
     one_b = take_b(0, "b1")
     pair_b = product_once(total, one_b) + total_b
     mine_b[1] = pair_b.astype(BF16)
+    hop("b2", "start")
     hop("b4", "start")
-    hop("b2", "start")
 
     @pl.when(plane <= 1)
     def _():
@@ -444,10 +452,10 @@
     lanes = pl.ds(pl.multiple_of(place * D, D), D)
     halves = [slice(h * D // PIECES, (h + 1) * D // PIECES) for h in range(PIECES)]
     for h, rows in enumerate(halves):
-        for n in chunks:
-            heads_out = product(reach[n, rows, :], state) + direct[n, rows, :]
-            scale = lax.rsqrt(jnp.mean(heads_out * heads_out, axis=-1, keepdims=True) + 1e-06)
-            back[n, rows, :] = (heads_out * scale * own[n, rows, :]).astype(BF16)
+        heads_out = product(reach[:, rows, :].reshape(-1, 2 * D), state) + direct[:, rows, :].reshape(-1, D)
+        scale = lax.rsqrt(jnp.mean(heads_out * heads_out, axis=-1, keepdims=True) + 1e-06)
+        gated = heads_out * scale * own[:, rows, :].reshape(-1, D)
+        back[:, rows, :] = gated.astype(BF16).reshape(PLANE, -1, D)
         for r in range(1, PLANE):
             dest = peer(r)
             send(
@@ -532,7 +540,7 @@
             dma((PIECES, PLANE - 1)), dma((PIECES, PLANE)),
             dma((PIECES, HEADS_X - 1)), dma((PIECES, HEADS_X - 1)),
             dma, dma((6,)), dma((4, PLANE)),
-            pltpu.SemaphoreType.REGULAR((4,)),
+            pltpu.SemaphoreType.REGULAR((5,)),
         ],
         compiler_params=pltpu.CompilerParams(
             collective_id=0, has_side_effects=True, vmem_limit_bytes=60 * 1024 * 1024

time: 44.3 us -> 42.1 us (0.950)
  Pallas kernels: 42.7 us -> 40.5 us
    pallas_call x1, Pallas kernels: 42.7 us -> 40.5 us  [on_device(): pl.pallas_call(kernel, out_shape=jax.ShapeDtypeStruct((tok, width), BF16)...]
where the time goes in v4:
time: 42.1 us; the launch traced here: 42 us
  Pallas kernels  40.5 us (96%)
  local copies, waits for them, and re-layouts  1.57 us (4%)
    pallas_call x1, Pallas kernels, on_device(): pl.pallas_call(kernel, out_shape=jax.ShapeDtypeStruct((tok, width), BF16)...  40.5 us
    unnamed x1, local copies, waits for them, and re-layouts  1.57 us

profile of v4, /device:TPU:161, one launch (start us, length us, event | category | flops | bytes accessed | tf_op | source)
XLA Modules:
  0.0 42.0 jit_solution(15843667257682632026)
XLA Ops:
  0.0 40.5 %shard_map.109 = bf16[128,512]{1,0:T(8,128)(2,1)} custom-call(bf16[128,512]{1,0:T(8,128)(2,1)} %q_ref.1, bf16[128,512]{1,0:T(8,128)(2,1)} %k_ref.1, bf16[128,1024]{1,0:T(8,128)(2,1)} %v_ref.1, bf16[128,1024]{1,0:T(8,128)(2,1)} %z_ref.1, f32[8,128]{1,0:T(8,128)} %bitcast.3, f32[8,128]{1,0:T(8,128)} %bitcast.4, f32[4,512]{1,0:T(4,128)} %cq_ref.1, ...), custom_call_target="tpu_custom_call" | custom-call | tf_op jit(solution)/shard_map/pallas_call | solution.py:507
  40.5 1.6 %copy.13 = bf16[128,512]{1,0:T(8,128)(2,1)} copy(bf16[128,512]{1,0:T(8,128)(2,1)} %shard_map.109) | data formatting | bytes 262144

commit v5 on v4

--- a/solution.py
+++ b/solution.py
@@ -111,7 +111,7 @@
 def kernel(
     q_ref, k_ref, v_ref, z_ref, decay_ref, rate_ref, cq_ref, ck_ref, cv_ref, gain_ref, w_ref, out_ref,
     blocks, raw, gate_own, gate_tiles, gates, halo, ext, act, taps, gain, reach, direct,
-    mine_m, got_m, mine_b, got_b, own, back, whole, w_all, x_send, x_got,
+    mine_m, got_m, mine_b, got_b, mid_b, own, back, whole, w_all, x_send, x_got,
     send_raw, recv_raw, send_gate, recv_gate, send_halo, recv_halo, send_m, recv_m, send_b, recv_b,
     send_back, recv_back, send_x, recv_x, w_sem, small_sem, block_sem, known,
 ):
@@ -156,7 +156,9 @@
     def tell(sem, r):
         pl.semaphore_signal(sem, inc=1, device_id=(plane_at(r) + place, head), device_id_type=MESH)
 
-    tell(barrier, -1)
+    @pl.when(plane > 0)
+    def _():
+        tell(barrier, -1)
 
     @pl.when(jnp.logical_and(plane > 0, jnp.logical_not(last)))
     def _():
@@ -189,7 +191,7 @@
             copy.wait()
 
     after = plane < PLANES - 1
-    pl.semaphore_wait(barrier, len(near) + 1 + jnp.where(jnp.logical_and(last, after), PLANE - 1, 0))
+    pl.semaphore_wait(barrier, len(near) + jnp.where(after, 1 + jnp.where(last, PLANE - 1, 0), 0))
 
     sent = []
 
@@ -231,10 +233,6 @@
         send(gate_tiles.at[dest], gates.at[place], send_gate.at[r - 1], recv_gate.at[place], (first + dest, head))
     raw_send(0)
     raw_send(1)
-
-    @pl.when(plane == PLANES - 1)
-    def _():
-        tell(known.at[4], 1)
 
     for a, copy in local:
         if a >= 2:
@@ -296,15 +294,6 @@
         tell(known.at[0], -1)
         tell(known.at[1], 1)
 
-    @pl.when(plane == PLANES - 1)
-    def _():
-        tell(known.at[3], 1)
-
-    @pl.when(plane == 0)
-    def _():
-        pl.semaphore_wait(known.at[4], 1)
-        tell(known.at[3], 1)
-
     activate(0)
     keys = [act[0, n] for n in chunks]
     keys_t = [keys[n].T for n in chunks]
@@ -353,11 +342,9 @@
     hops = {
         "m1": (m_copy(0, 0, 1), 1, 6),
         "m2": (m_copy(1, 1, 2), 2, 5),
-        "m4": (m_copy(1, 2, 4), 2, 3),
         "b1": (b_copy(0, 0, 1), 0, 6),
         "b2": (b_copy(1, 1, 2), 0, 5),
-        "b4": (b_copy(1, 2, 4), 0, 3),
-        "b6": (b_copy(1, 3, 6), 0, 1),
+        "b4": (b_copy(2, 2, 4), 0, 3),
     }
 
     def hop(name, act_on):
@@ -407,19 +394,6 @@
         pl.semaphore_wait(known.at[2], 1)
 
     hop("m2", "start")
-    hop("m4", "start")
-    one_b = take_b(0, "b1")
-    pair_b = product_once(total, one_b) + total_b
-    mine_b[1] = pair_b.astype(BF16)
-    hop("b2", "start")
-    hop("b4", "start")
-
-    @pl.when(plane <= 1)
-    def _():
-        pl.semaphore_wait(known.at[3], 1)
-
-    hop("b6", "start")
-
     prefix = {1: maps[0], 2: two[0], 4: four[0]}
     prefix_b = {1: offsets[0], 2: two_b[0], 4: four_b[0]}
     for n, later, later_b, earlier in (
@@ -438,15 +412,32 @@
         )
         reach[n] = left(through[:, :D] + prefix[n][0] * response[n])
         direct[n] = through[:, D:] + seen[n]
+    one_b = take_b(0, "b1")
+    pair_b = product_once(total, one_b) + total_b
+    mine_b[1] = pair_b.astype(BF16)
+    hop("b2", "start")
+
+    mid_b[...] = jnp.zeros_like(mid_b)
+
+    @pl.when(jnp.logical_and(plane >= 2, plane <= 3))
+    def _():
+        hops["b2"][0].wait_recv()
+        mid_b[...] = got_b[1]
+
+    mine_b[2] = (product_once(pair, mid_b[...]) + pair_b).astype(BF16)
+    hop("b4", "start")
+
     raw_arrived(3)
     for n in chunks:
         own[n] = silu(raw[3, n].astype(F32)) * gain[...]
 
+    @pl.when(plane >= 4)
+    def _():
+        hops["b2"][0].wait_recv()
+
     two_back = join(one, take_m(1, "m2"))
-    four_back = join(two_back, take_m(2, "m4"))
-    state = one_b.astype(F32)
-    for linear, slot, name in ((one, 1, "b2"), (two_back, 2, "b4"), (four_back, 3, "b6")):
-        state = state + product_once(linear, take_b(slot, name))
+    state = one_b.astype(F32) + product_once(one, jnp.where(plane >= 2, got_b[1].astype(F32), 0.0).astype(BF16))
+    state = state + product_once(two_back, take_b(2, "b4"))
     state = right(state)
 
     lanes = pl.ds(pl.multiple_of(place * D, D), D)
@@ -523,9 +514,10 @@
             VMEM((PLANE, D, 2 * D), BF16),
             VMEM((PLANE, D, D), F32),
             VMEM((2, D + 16, D), BF16),
-            VMEM((3, D + 16, D), BF16),
-            VMEM((2, D, D), BF16),
-            VMEM((4, D, D), BF16),
+            VMEM((2, D + 16, D), BF16),
+            VMEM((3, D, D), BF16),
+            VMEM((3, D, D), BF16),
+            VMEM((D, D), BF16),
             VMEM((PLANE, D, D), F32),
             VMEM((PLANE, D, D), BF16),
             VMEM((tok, PLANE * D), BF16),
@@ -535,12 +527,12 @@
             dma((4, PLANE - 1)), dma((4, PLANE)),
             dma((PLANE - 1,)), dma((PLANE,)),
             dma((3, PLANE)), dma((3,)),
+            dma((2,)), dma((2,)),
             dma((3,)), dma((3,)),
-            dma((4,)), dma((4,)),
             dma((PIECES, PLANE - 1)), dma((PIECES, PLANE)),
             dma((PIECES, HEADS_X - 1)), dma((PIECES, HEADS_X - 1)),
             dma, dma((6,)), dma((4, PLANE)),
-            pltpu.SemaphoreType.REGULAR((5,)),
+            pltpu.SemaphoreType.REGULAR((3,)),
         ],
         compiler_params=pltpu.CompilerParams(
             collective_id=0, has_side_effects=True, vmem_limit_bytes=60 * 1024 * 1024

time: 42.1 us -> 41.9 us (level)
  no operation moved by 1% of the time
where the time goes in v5:
time: 41.9 us; the launch traced here: 41.8 us
  Pallas kernels  40.2 us (96%)
  local copies, waits for them, and re-layouts  1.57 us (4%)
    pallas_call x1, Pallas kernels, on_device(): pl.pallas_call(kernel, out_shape=jax.ShapeDtypeStruct((tok, width), BF16)...  40.2 us
    unnamed x1, local copies, waits for them, and re-layouts  1.57 us

profile of v5, /device:TPU:161, one launch (start us, length us, event | category | flops | bytes accessed | tf_op | source)
XLA Modules:
  0.0 41.8 jit_solution(13321319062432655910)
XLA Ops:
  0.0 40.2 %shard_map.109 = bf16[128,512]{1,0:T(8,128)(2,1)} custom-call(bf16[128,512]{1,0:T(8,128)(2,1)} %q_ref.1, bf16[128,512]{1,0:T(8,128)(2,1)} %k_ref.1, bf16[128,1024]{1,0:T(8,128)(2,1)} %v_ref.1, bf16[128,1024]{1,0:T(8,128)(2,1)} %z_ref.1, f32[8,128]{1,0:T(8,128)} %bitcast.3, f32[8,128]{1,0:T(8,128)} %bitcast.4, f32[4,512]{1,0:T(4,128)} %cq_ref.1, ...), custom_call_target="tpu_custom_call" | custom-call | tf_op jit(solution)/shard_map/pallas_call | solution.py:498
  40.2 1.6 %copy.13 = bf16[128,512]{1,0:T(8,128)(2,1)} copy(bf16[128,512]{1,0:T(8,128)(2,1)} %shard_map.109) | data formatting | bytes 262144

commit v6 on v5

--- a/solution.py
+++ b/solution.py
@@ -11,7 +11,8 @@
 PLANE = 8
 PLANES = 8
 HEADS_X = 4
-PIECES = 4
+ROWS = (0, 32, 80, 128)
+PIECES = len(ROWS) - 1
 MESH = pl.DeviceIdType.MESH
 VMEM = pltpu.VMEM
 
@@ -131,6 +132,23 @@
     def columns(a, dest):
         return pl.ds(pl.multiple_of((dest if a % 2 else dest // 2) * D, D), D)
 
+    barrier = pltpu.get_barrier_semaphore()
+    near = [(first + peer(r), head) for r in range(1, PLANE)]
+    near += [(me, lax.rem(head + r, HEADS_X)) for r in range(1, HEADS_X)]
+    for device in near:
+        pl.semaphore_signal(barrier, inc=1, device_id=device, device_id_type=MESH)
+
+    def tell(sem, r):
+        pl.semaphore_signal(sem, inc=1, device_id=(plane_at(r) + place, head), device_id_type=MESH)
+
+    @pl.when(plane > 0)
+    def _():
+        tell(barrier, -1)
+
+    @pl.when(jnp.logical_and(plane > 0, jnp.logical_not(last)))
+    def _():
+        pl.semaphore_signal(barrier, inc=1, device_id=(plane_at(-1) + PLANE - 1, head), device_id_type=MESH)
+
     small = [
         pltpu.make_async_copy(src, dst, small_sem.at[i])
         for i, (src, dst) in enumerate(
@@ -146,23 +164,6 @@
     ]
     for copy in small:
         copy.start()
-
-    barrier = pltpu.get_barrier_semaphore()
-    near = [(first + peer(r), head) for r in range(1, PLANE)]
-    near += [(me, lax.rem(head + r, HEADS_X)) for r in range(1, HEADS_X)]
-    for device in near:
-        pl.semaphore_signal(barrier, inc=1, device_id=device, device_id_type=MESH)
-
-    def tell(sem, r):
-        pl.semaphore_signal(sem, inc=1, device_id=(plane_at(r) + place, head), device_id_type=MESH)
-
-    @pl.when(plane > 0)
-    def _():
-        tell(barrier, -1)
-
-    @pl.when(jnp.logical_and(plane > 0, jnp.logical_not(last)))
-    def _():
-        pl.semaphore_signal(barrier, inc=1, device_id=(plane_at(-1) + PLANE - 1, head), device_id_type=MESH)
 
     local = []
     kept = []
@@ -441,7 +442,7 @@
     state = right(state)
 
     lanes = pl.ds(pl.multiple_of(place * D, D), D)
-    halves = [slice(h * D // PIECES, (h + 1) * D // PIECES) for h in range(PIECES)]
+    halves = [slice(ROWS[h], ROWS[h + 1]) for h in range(PIECES)]
     for h, rows in enumerate(halves):
         heads_out = product(reach[:, rows, :].reshape(-1, 2 * D), state) + direct[:, rows, :].reshape(-1, D)
         scale = lax.rsqrt(jnp.mean(heads_out * heads_out, axis=-1, keepdims=True) + 1e-06)

time: 41.9 us -> 41.7 us (level)
  no operation moved by 1% of the time
where the time goes in v6:
time: 41.7 us; the launch traced here: 41.6 us
  Pallas kernels  40 us (96%)
  local copies, waits for them, and re-layouts  1.57 us (4%)
    pallas_call x1, Pallas kernels, on_device(): pl.pallas_call(kernel, out_shape=jax.ShapeDtypeStruct((tok, width), BF16)...  40 us
    unnamed x1, local copies, waits for them, and re-layouts  1.57 us

profile of v6, /device:TPU:161, one launch (start us, length us, event | category | flops | bytes accessed | tf_op | source)
XLA Modules:
  0.0 41.6 jit_solution(11325264710960696535)
XLA Ops:
  0.0 40.0 %shard_map.109 = bf16[128,512]{1,0:T(8,128)(2,1)} custom-call(bf16[128,512]{1,0:T(8,128)(2,1)} %q_ref.1, bf16[128,512]{1,0:T(8,128)(2,1)} %k_ref.1, bf16[128,1024]{1,0:T(8,128)(2,1)} %v_ref.1, bf16[128,1024]{1,0:T(8,128)(2,1)} %z_ref.1, f32[8,128]{1,0:T(8,128)} %bitcast.3, f32[8,128]{1,0:T(8,128)} %bitcast.4, f32[4,512]{1,0:T(4,128)} %cq_ref.1, ...), custom_call_target="tpu_custom_call" | custom-call | tf_op jit(solution)/shard_map/pallas_call | solution.py:499
  40.0 1.6 %copy.13 = bf16[128,512]{1,0:T(8,128)(2,1)} copy(bf16[128,512]{1,0:T(8,128)(2,1)} %shard_map.109) | data formatting | bytes 262144

commit v7 on v6

--- a/solution.py
+++ b/solution.py
@@ -315,6 +315,8 @@
     def _():
         tell(known.at[2], -2)
 
+    raw_arrived(1)
+    activate(1)
     solved_k = [right(product(inverse[n], right((rate_col[n] * growth[n]) * keys[n]))) for n in chunks]
     maps = []
     for n in chunks:
@@ -369,8 +371,6 @@
     put_m(0, total)
     hop("m1", "start")
 
-    raw_arrived(1)
-    activate(1)
     solved_v = [right(product(inverse[n], right(rate_col[n] * act[1, n]))) for n in chunks]
     offsets = [product(weighted[n], solved_v[n]) for n in chunks]
     two_b = [advance(maps[n + 1], offsets[n + 1], offsets[n]) for n in range(0, PLANE, 2)]
@@ -474,23 +474,27 @@
             )
     weights = w_all[:, pl.ds(pl.multiple_of(head * width, width), width)]
     share = jnp.dot(whole[...], weights, preferred_element_type=F32)
+    early = len(sent) - PIECES * (HEADS_X - 1)
+    for copy in sent[:early]:
+        copy.wait_send()
+
+    for name in hops:
+        hop(name, "wait_send")
+
+    @pl.when(jnp.logical_and(last, after))
+    def _():
+        for a in range(3):
+            for j in range(PLANE):
+                halo_copy(a, j).wait_send()
+
     for h, rows in enumerate(halves):
         part = share[rows]
         for r in (1, 3, 2):
             arrived(x_got.at[r - 1, rows, :], send_x.at[h, r - 1], recv_x.at[h, r - 1])
             part = part + x_got[r - 1, rows, :].astype(F32)
         out_ref[rows, :] = part.astype(BF16)
-    for copy in sent:
+    for copy in sent[early:]:
         copy.wait_send()
-
-    for name in hops:
-        hop(name, "wait_send")
-
-    @pl.when(jnp.logical_and(last, after))
-    def _():
-        for a in range(3):
-            for j in range(PLANE):
-                halo_copy(a, j).wait_send()
 
 
 def on_device(q_in, k_in, v_in, z_gate, decay, rate, conv_q, conv_k, conv_v, norm_gain, w_out):

time: 41.7 us -> 41.5 us (level)
  no operation moved by 1% of the time
where the time goes in v7:
time: 41.5 us
  Pallas kernels  39.9 us (96%)
  local copies, waits for them, and re-layouts  1.57 us (4%)
    pallas_call x1, Pallas kernels, on_device(): pl.pallas_call(kernel, out_shape=jax.ShapeDtypeStruct((tok, width), BF16)...  39.9 us
    unnamed x1, local copies, waits for them, and re-layouts  1.57 us

profile of v7, /device:TPU:161, one launch (start us, length us, event | category | flops | bytes accessed | tf_op | source)
XLA Modules:
  0.0 41.5 jit_solution(11268803468540146983)
XLA Ops:
  0.0 39.9 %shard_map.109 = bf16[128,512]{1,0:T(8,128)(2,1)} custom-call(bf16[128,512]{1,0:T(8,128)(2,1)} %q_ref.1, bf16[128,512]{1,0:T(8,128)(2,1)} %k_ref.1, bf16[128,1024]{1,0:T(8,128)(2,1)} %v_ref.1, bf16[128,1024]{1,0:T(8,128)(2,1)} %z_ref.1, f32[8,128]{1,0:T(8,128)} %bitcast.3, f32[8,128]{1,0:T(8,128)} %bitcast.4, f32[4,512]{1,0:T(4,128)} %cq_ref.1, ...), custom_call_target="tpu_custom_call" | custom-call | tf_op jit(solution)/shard_map/pallas_call | solution.py:503
  39.9 1.6 %copy.13 = bf16[128,512]{1,0:T(8,128)(2,1)} copy(bf16[128,512]{1,0:T(8,128)(2,1)} %shard_map.109) | data formatting | bytes 262144
